TPU v7x, 256 devices: a whole 4x4x8 slice. The times are simulated.
256 devices in a mesh: seq: 128 (over x_hi, z, y, core), head: 2 (over x_lo).
Axes of the slice: x: 4 (x_hi: 2, x_lo: 2; x = x_hi * 2 + x_lo), y: 4, z: 8, core: 2. Of those that a mesh axis runs over, the one named last changes fastest.
Arguments:
- inputs: bfloat16 [256, 128, 1152], P('seq'), may hold values from -8 to 8, as said below
- out_grad: bfloat16 [256, 128, 1152], P('seq'), may hold values from -6 to 6
- gate: float32 [1152], replicated, may hold values from -4 to 4
- qkv_weight: bfloat16 [1152, 3, 1152], P('seq', None, 'head'), as said below
- out_weight: bfloat16 [1152, 1152], P('seq', 'head'), may hold values from -0.1875 to 0.1875
Outputs:
- grad_inputs: bfloat16 [256, 128, 1152], P('seq')
- grad_qkv: float32 [1152, 3, 1152], P('seq', None, 'head')
- grad_out: float32 [1152, 1152], P('seq', 'head')
Inputs may be any that keep to these rules, and one draw needn't show every extreme that they name: `inputs`: entries of the input tokens lie in this range. `qkv_weight`: entries lie within six times the fan-in scale 1 / sqrt(1152).
All inputs are finite; a program needn't handle non-finite values.
Results may differ from a plain program's by a relative error of at most 0.03.
The roundings to bfloat16 on the way count: a program that leaves them out, or rounds other values in their place, can miss the bound.
Values may be sent and summed in bfloat16 or wider, within the bound.
A program may use at most 128 MiB of HBM per device.

v0:
```python
import jax
import jax.numpy as jnp
from jax import lax
from jax.sharding import PartitionSpec as P

HEAD_DIM = 72
FRAMES = 32


def layer_norm(flat):
    mean = jnp.mean(flat, -1, keepdims=True)
    centered = flat - mean
    rstd = lax.rsqrt(jnp.mean(centered * centered, -1, keepdims=True) + 1e-06)
    return (centered * rstd, rstd)


def attention_backward(qkv_block, dout):
    frames_all, places, three, columns = qkv_block.shape
    heads_here = columns // HEAD_DIM
    clips_here = frames_all // FRAMES
    shape_five = (clips_here, FRAMES, places, heads_here, HEAD_DIM)
    query = qkv_block[:, :, 0].reshape(shape_five)
    keyed = qkv_block[:, :, 1].reshape(shape_five)
    value = qkv_block[:, :, 2].reshape(shape_five)
    dgrad = dout.reshape(shape_five)
    scale = HEAD_DIM ** (-0.5)
    scores = (
        jnp.einsum("cfphe,cgphe->cphfg", query, keyed, preferred_element_type=jnp.float32) * scale
    )
    probs = jax.nn.softmax(scores, axis=-1)
    probs_b = probs.astype(jnp.bfloat16)
    attended = jnp.einsum(
        "cphfg,cgphe->cfphe", probs_b, value, preferred_element_type=jnp.float32
    ).astype(jnp.bfloat16)
    dprobs = jnp.einsum("cfphe,cgphe->cphfg", dgrad, value, preferred_element_type=jnp.float32)
    delta = jnp.einsum("cfphe,cfphe->cphf", dgrad.astype(jnp.float32), attended.astype(jnp.float32))
    dscores = (probs * (dprobs - delta[..., None]) * scale).astype(jnp.bfloat16)
    grad_q = jnp.einsum(
        "cphfg,cgphe->cfphe", dscores, keyed, preferred_element_type=jnp.float32
    ).astype(jnp.bfloat16)
    grad_k = jnp.einsum(
        "cphfg,cfphe->cgphe", dscores, query, preferred_element_type=jnp.float32
    ).astype(jnp.bfloat16)
    grad_v = jnp.einsum(
        "cphfg,cfphe->cgphe", probs_b, dgrad, preferred_element_type=jnp.float32
    ).astype(jnp.bfloat16)
    stacked = jnp.stack([grad_q, grad_k, grad_v, attended], 5)
    stacked = jnp.moveaxis(stacked, 5, 3)
    return stacked.reshape(frames_all, places, 4, columns)


def finish_grads(normed, gated, dqkv, attended, w_flat, own_rows, columns):
    part = normed
    term = lax.dot_general(part, dqkv, (((0,), (0,)), ((), ())), preferred_element_type=jnp.float32)
    grad_qkv = lax.psum_scatter(
        term.reshape(lax.axis_size("seq") * own_rows, 3, columns),
        "seq",
        scatter_dimension=0,
        tiled=True,
    )
    part = gated
    grad_out = lax.psum_scatter(
        lax.dot_general(
            part, attended, (((0,), (0,)), ((), ())), preferred_element_type=jnp.float32
        ),
        "seq",
        scatter_dimension=0,
        tiled=True,
    )
    partial_sum = lax.dot_general(
        dqkv, w_flat, (((1,), (1,)), ((), ())), preferred_element_type=jnp.float32
    )
    dnormed = lax.psum(partial_sum.astype(jnp.bfloat16), "head")
    return (dnormed, grad_qkv, grad_out)


def on_device(inputs, out_grad, gate, qkv_weight, out_weight):
    frames_here, positions, width = inputs.shape
    own_rows = qkv_weight.shape[0]
    columns = qkv_weight.shape[2]
    flat = inputs.reshape(-1, width).astype(jnp.float32)
    ghat, rstd = layer_norm(flat)
    normed = ghat.astype(jnp.bfloat16)
    up_flat = out_grad.reshape(-1, width)
    gated = (gate * up_flat.astype(jnp.float32)).astype(jnp.bfloat16)
    w_all, wo_all = (
        lax.all_gather(qkv_weight, "seq", axis=0, tiled=True),
        lax.all_gather(out_weight, "seq", axis=0, tiled=True),
    )
    w_flat = w_all.reshape(width, 3 * columns)
    qkv = jnp.dot(normed, w_flat, preferred_element_type=jnp.float32).astype(jnp.bfloat16)
    qkv = qkv.reshape(frames_here, positions, 3, columns)
    dout = jnp.dot(gated, wo_all, preferred_element_type=jnp.float32).astype(jnp.bfloat16)
    dout = dout.reshape(frames_here, positions, 1, columns)
    moved = lax.all_to_all(
        jnp.concatenate([qkv, dout], 2), "seq", split_axis=1, concat_axis=0, tiled=True
    )
    grads = attention_backward(moved[:, :, 0:3], moved[:, :, 3])
    back = lax.all_to_all(grads, "seq", split_axis=0, concat_axis=1, tiled=True)
    dqkv = back[:, :, 0:3].reshape(-1, 3 * columns)
    attended = back[:, :, 3].reshape(-1, columns)
    dnormed, grad_qkv, grad_out = finish_grads(
        normed, gated, dqkv, attended, w_flat, own_rows, columns
    )
    dfloat = dnormed.astype(jnp.float32)
    mean_one = jnp.mean(dfloat, -1, keepdims=True)
    mean_two = jnp.mean(dfloat * ghat, -1, keepdims=True)
    result = up_flat.astype(jnp.float32) + rstd * (dfloat - mean_one - ghat * mean_two)
    grad_inputs = result.astype(jnp.bfloat16).reshape(frames_here, positions, width)
    return (grad_inputs, grad_qkv, grad_out)


def solution(mesh):
    in_specs = (
        P("seq", None, None),
        P("seq", None, None),
        P(),
        P("seq", None, "head"),
        P("seq", "head"),
    )
    out_specs = (P("seq", None, None), P("seq", None, "head"), P("seq", "head"))
    return jax.shard_map(
        on_device, mesh=mesh, in_specs=in_specs, out_specs=out_specs, check_vma=False
    )
```

profile of v0, /device:TPU:1, one launch (start us, length us, event | category | flops | bytes accessed | tf_op | source)
XLA Modules:
  0.0 1746.4 jit_solution(17405475546019465976)
XLA Ops:
  9.9 1.4 multiply_reduce_fusion
  12.6 119.5 %all-gather.6.cloned.1.call-done = bf16[128,9,576]{2,1,0:T(8,128)(2,1)} async-done(((bf16[1,9,576]{2,1,0:T(8,128)(2,1)}), bf16[128,9,576]{2,1,0:T(8,128)(2,1)}) %all-gather.6.cloned.1.call-update) | async-done | bytes 1327120 | tf_op jit(solution)/shard_map/all_gather | solution.py:88
  132.2 3.0 reshape.185
  135.2 1.8 convolution_convert_fusion.6
  137.0 2.2 copy.53
  139.2 116.6 %all-gather.4.cloned.1.call-done = bf16[1152,3,576]{2,1,0:T(4,128)(2,1)} async-done(((bf16[9,3,576]{2,1,0:T(4,128)(2,1)}), bf16[1152,3,576]{2,1,0:T(4,128)(2,1)}) %all-gather.4.cloned.1.call-update) | async-done | bytes 3981328 | tf_op jit(solution)/shard_map/all_gather | solution.py:87
  255.8 11.3 copy.51
  267.1 3.5 convolution_convert_fusion
  270.8 2.0 copy.52
  272.8 2.5 pad_maximum_fusion
  275.3 46.8 %all_to_all.36 = bf16[2,128,4,576]{3,2,0,1:T(4,128)(2,1)S(1)} all-to-all(bf16[2,128,4,576]{3,2,0,1:T(4,128)(2,1)S(1)} %pad_maximum_fusion), channel_id=1, replica_groups=mesh['seq'=128,'head'=2] {'seq'}, dimensions={1} | all-to-all | bytes 2359296 | tf_op jit(solution)/shard_map/all_to_all | solution.py:95
  322.1 7.0 slice_reduce_fusion.1
  331.8 1.4 reshape.177
  333.2 1.6 fusion.43
  334.8 1.7 fusion.8
  339.8 3.3 reshape.190
  343.0 5.5 all-to-all-start.1
  349.6 36.9 %all-to-all-done.1 = bf16[256,1,4,576]{3,2,1,0:T(4,128)(2,1)S(1)} async-done(((bf16[256,1,4,576]{3,2,1,0:T(4,128)(2,1)}), bf16[256,1,4,576]{3,2,1,0:T(4,128)(2,1)S(1)}, u32[]{:S(2)}, u32[]{:S(2)}) %all-to-all-start.1) | async-done | bytes 1179680 | tf_op jit(solution)/shard_map/all_to_all | solution.py:99
  386.5 1.9 copy.67
  388.5 4.7 convolution_convert_fusion.1
  393.1 1.3 copy.123
  394.4 1.5 slice.33
  396.0 2.5 fusion.48
  398.5 17.5 copy.69
  416.0 1.4 copy.70
  417.4 2.3 fusion.26
  421.5 9.1 all-reduce.6.cloned.1.call-done
  430.6 1.6 convert_reduce_fusion
  432.2 1.3 fusion.12
  433.5 1303.3 %all-reduce.8.cloned.1.call-done = (f32[1152,3,576]{2,1,0:T(4,128)}, f32[1152,576]{1,0:T(8,128)}) async-done(((f32[1152,3,576]{2,1,0:T(4,128)}, f32[1152,576]{1,0:T(8,128)}), (f32[1152,3,576]{2,1,0:T(4,128)}, f32[1152,576]{1,0:T(8,128)})) %all-reduce.8.cloned.1.call-update) | async-done | bytes 10616848
  1736.9 1.5 constant_dynamic-slice_fusion.1
  1738.4 1.5 constant_dynamic-slice_fusion
  (52 shorter events, 12.6 us)
Async XLA Ops:
  7.2 4.1 copy-start
  7.2 4.4 copy-start.1
  7.2 4.4 copy-start.9
  7.2 125.0 %all-gather.6.cloned.1.call-start = ((), (), s32[]{:S(2)}) async-start(), calls=%async_computation.4 | async-start | bytes 2641920 | tf_op jit(solution)/shard_map/all_gather | solution.py:88
  7.9 247.9 %all-gather.4.cloned.1.call-start = ((), (), s32[]{:S(2)}) async-start(), calls=%async_computation.2 | async-start | bytes 5944320 | tf_op jit(solution)/shard_map/all_gather | solution.py:87
  11.6 255.5 %copy-start.4 = (bf16[2,128,1152]{2,1,0:T(8,128)(2,1)}, bf16[2,128,1152]{2,1,0:T(8,128)(2,1)S(1)}, u32[]{:S(2)}) copy-start(bf16[2,128,1152]{2,1,0:T(8,128)(2,1)S(1)} %multiply_convert_fusion) | copy-start | bytes 1769476
  334.7 1.7 copy-start.7
  334.8 1.7 copy-start.8
  334.8 2.0 copy-start.11
  343.0 43.5 %all-to-all-start.1 = ((bf16[256,1,4,576]{3,2,1,0:T(4,128)(2,1)}), bf16[256,1,4,576]{3,2,1,0:T(4,128)(2,1)S(1)}, u32[]{:S(2)}, u32[]{:S(2)}) async-start(bf16[256,1,4,576]{3,2,1,0:T(4,128)(2,1)} %reshape.190), calls=%async_computation.1 | async-start | bytes 2621440 | tf_op jit(solution)/shard_map/all_to_all | solution.py:99
  348.6 82.0 %all-reduce.6.cloned.1.call-start = ((), (), s32[]{:S(2)}) async-start(), calls=%async_computation.3 | async-start | bytes 1179648 | tf_op jit(solution)/shard_map/psum | solution.py:73
  388.5 4.7 copy-start.2
  396.0 1340.9 %all-reduce.8.cloned.1.call-start = ((), (), s32[]{:S(2)}) async-start(), calls=%async_computation.5 | async-start | bytes 29491200
  398.5 17.5 %copy-start.3 = (bf16[2,128,1,576]{3,2,0,1:T(2,128)(2,1)S(1)}, bf16[2,128,1,576]{3,2,0,1:T(2,128)(2,1)}, u32[]{:S(2)}) copy-start(bf16[2,128,1,576]{3,2,0,1:T(2,128)(2,1)} %slice.33) | copy-start | bytes 884740
  416.0 1.4 copy-start.6
  419.6 0.7 copy-start.10
  430.6 1.6 copy-start.5
Sparse Core Ops, SparseCore 0:
  11.6 120.4 all-gather.5
  135.9 119.7 all-gather.3
  396.1 34.5 all-reduce.5
  433.4 1303.3 all-reduce.7
where the time goes:
time: 1750 us
  waiting for transfers between devices  1590 us (91%)
  local copies, waits for them, and re-layouts  61 us (3%)
  blocking collectives  46.8 us (3%)
  matrix products  19.5 us (1%)
    unnamed x5, waiting for transfers between devices  1300 us
    all_gather x1, waiting for transfers between devices, on_device(): lax.all_gather(out_weight, 'seq', axis=0, tiled=True)  120 us
    all_gather x1, waiting for transfers between devices, on_device(): lax.all_gather(qkv_weight, 'seq', axis=0, tiled=True)  117 us
    all_to_all x1, blocking collectives, on_device(): lax.all_to_all(jnp.concatenate([qkv, dout], 2), 'seq', split_axis=1, conc...  46.8 us
    all_to_all x1, waiting for transfers between devices, on_device(): back = lax.all_to_all(grads, 'seq', split_axis=0, concat_axis=1, tiled=True)  36.9 us
  transfers between devices with their start and end apart: 5, of which 5 were waited for; matrix products, arithmetic and copies ran while one was open for 2% of the time, Pallas kernels for 0%

commit v1 on v0

v1 whole, which is shorter than its diff:
```python
import functools

import jax
import jax.numpy as jnp
from jax import lax
from jax.experimental import pallas as pl
from jax.experimental.pallas import tpu as pltpu
from jax.sharding import PartitionSpec as P

D = 1152
HEAD_DIM = 72
XS, ZS, YS = 2, 8, 4
CHIPS = XS * ZS * YS
BLK = 1408
MESH = pl.DeviceIdType.MESH
BF = jnp.bfloat16
F32 = jnp.float32
VMEM_BYTES = 58 * 2**20


def place():
    s = lax.axis_index("seq")
    h = lax.axis_index("head")
    return s // 64, (s // 8) % 8, (s // 2) % 4, s % 2, h


def seq_of(x, z, y, core):
    return ((x * 8 + z) * 4 + y) * 2 + core


def signal(sem, target):
    pl.semaphore_signal(sem, inc=1, device_id=target, device_id_type=MESH)


def remote(src, dst, send, recv, target):
    return pltpu.make_async_remote_copy(
        src_ref=src, dst_ref=dst, send_sem=send, recv_sem=recv, device_id=target, device_id_type=MESH
    )


def permuted_feature(shape, dim):
    f = lax.broadcasted_iota(jnp.int32, shape, dim)
    owner = f // 9
    q = f - owner * 9
    return jnp.where(q < 8, owner * 8 + q, 1024 + (owner % 2) * 64 + owner // 2)


def gather_kernel(
    in_ref, up_ref, wsh_ref, buf, xin,
    sib_v, mine_v, xg_v, perm_v,
    sib_sem, z_send, z_recv, x_sem, y_send, y_recv, t_send, t_recv, s_sem, l_sem,
):
    x, z, y, core, h = place()
    ck = (z % 2) * 4 + y
    sibling = (seq_of(x, z, y, 1 - core), h)
    x_peer = (seq_of(1 - x, z, y, core), h)
    z_peers = [(seq_of(x, (z + d) % 8, y, core), h) for d in range(1, 8)]
    y_peers = [(seq_of(x, z, (y + d) % 4, core), h) for d in range(1, 4)]
    t_chips = [(ck + d) % 8 for d in range(1, 8)]
    t_peers = [(seq_of(x, (z // 2) * 2 + c // 4, c % 4, core), h) for c in t_chips]
    everyone = [sibling, x_peer] + z_peers + y_peers + t_peers
    barrier = pltpu.get_barrier_semaphore()
    for peer in everyone:
        signal(barrier, peer)
    pl.semaphore_wait(barrier, len(everyone))

    swap = remote(wsh_ref.at[1 - core], sib_v, sib_sem.at[0], sib_sem.at[1], sibling)
    swap.start()
    swap.wait()
    mine_v[...] = wsh_ref[core] + sib_v[...]
    z_copies = [
        remote(mine_v, buf.at[x, z, y], z_send.at[d], z_recv.at[d], z_peers[d]) for d in range(7)
    ]
    for c in z_copies:
        c.start()
    own = pltpu.make_async_copy(mine_v, buf.at[x, z, y], l_sem.at[0])
    own.start()

    row = permuted_feature((D, 1), 0)
    col = lax.broadcasted_iota(jnp.int32, (1, D), 1)
    perm_v[...] = jnp.where(row == col, 1.0, 0.0).astype(BF)
    for i, ref in enumerate((in_ref, up_ref)):
        p = jnp.dot(ref[...].reshape(256, D), perm_v[...], preferred_element_type=F32)
        for g in range(16):
            part = jnp.concatenate([p[8 * g : 8 * g + 8], p[128 + 8 * g : 136 + 8 * g]], 0)
            xg_v[g, :, i * D : (i + 1) * D] = part.astype(BF)
    t_copies = [
        remote(
            xg_v.at[pl.ds(2 * t_chips[d], 2)], xin.at[:, ck, core],
            t_send.at[d], t_recv.at[d], t_peers[d],
        )
        for d in range(7)
    ]
    for c in t_copies:
        c.start()
    own_t = pltpu.make_async_copy(xg_v.at[pl.ds(2 * ck, 2)], xin.at[:, ck, core], l_sem.at[1])
    own_t.start()

    own.wait()
    for c in z_copies:
        c.wait()
    x_copy = remote(buf.at[x, :, y], buf.at[x, :, y], x_sem.at[0], x_sem.at[1], x_peer)
    x_copy.start()
    y_one = [
        remote(buf.at[x, :, y], buf.at[x, :, y], y_send.at[d], y_recv.at[d], y_peers[d])
        for d in range(3)
    ]
    for c in y_one:
        c.start()
    x_copy.wait()
    y_two = [
        remote(
            buf.at[1 - x, :, y], buf.at[1 - x, :, y], y_send.at[3 + d], y_recv.at[3 + d], y_peers[d]
        )
        for d in range(3)
    ]
    for c in y_two:
        c.start()
    own_t.wait()
    for c in t_copies:
        c.wait()
    s_copy = remote(xin.at[:, :, core], xin.at[:, :, core], s_sem.at[0], s_sem.at[1], sibling)
    s_copy.start()
    for c in y_one + y_two:
        c.wait()
    s_copy.wait()


def normalise(v):
    mean = jnp.mean(v, -1, keepdims=True)
    centered = v - mean
    rstd = lax.rsqrt(jnp.mean(centered * centered, -1, keepdims=True) + 1e-06)
    return centered * rstd, rstd


def turn(v, by):
    return jnp.concatenate([v[:, -by:], v[:, :-by]], 1)


def nt(a, b):
    return lax.dot_general(a, b, (((1,), (1,)), ((), ())), preferred_element_type=F32)


def tn(a, b):
    return lax.dot_general(a, b, (((0,), (0,)), ((), ())), preferred_element_type=F32)


def attention(qa, ka, va, da):
    scale = HEAD_DIM ** (-0.5)
    rows = lax.broadcasted_iota(jnp.int32, (256, 256), 0)
    cols = lax.broadcasted_iota(jnp.int32, (256, 256), 1)
    same = (rows & 7) == (cols & 7)
    outs = [[[] for _ in range(3)] for _ in range(4)]
    for head, (lo, hi) in enumerate(((0, 128), (0, 256), (128, 256), (128, 384))):
        lane = lax.broadcasted_iota(jnp.int32, (1, hi - lo), 1) + lo
        keep = (lane >= HEAD_DIM * head) & (lane < HEAD_DIM * (head + 1))
        q, k, v, d = (a[:, lo:hi] for a in (qa, ka, va, da))
        qm = jnp.where(keep, q, jnp.zeros_like(q))
        dm = jnp.where(keep, d, jnp.zeros_like(d))
        scores = jnp.where(same, nt(qm, k) * scale, -1e30)
        top = jnp.max(scores, -1, keepdims=True)
        e = jnp.exp(scores - top)
        probs = e / jnp.sum(e, -1, keepdims=True)
        probs_b = probs.astype(BF)
        att = jnp.dot(probs_b, v, preferred_element_type=F32).astype(BF)
        delta = jnp.sum(dm.astype(F32) * att.astype(F32), -1, keepdims=True)
        ds = (probs * (nt(dm, v) - delta) * scale).astype(BF)
        dq = jnp.dot(ds, k, preferred_element_type=F32)
        dk = tn(ds, q)
        dv = tn(probs_b, d)
        for slot, val in zip(outs, (dq, dk, dv, att.astype(F32))):
            val = jnp.where(keep, val, 0.0)
            for t in range(lo // 128, hi // 128):
                slot[t].append(val[:, t * 128 - lo : t * 128 - lo + 128])
    return [jnp.concatenate([functools.reduce(lambda a, b: a + b, t) for t in s], 1) for s in outs]


def compute_kernel(buf, xin, gate_ref, dw, dn, w_v, norm_v, dz_v, g_v, f_v):
    w_v[0:1024, :] = buf[:, :, 0:D].reshape(1024, D)
    for r in range(2):
        f_v[...] = buf[:, :, D + 128 * r : D + 128 * (r + 1)].reshape(1024, 128).astype(F32)
        for j in range(9):
            w_v[1024 + 64 * r : 1088 + 64 * r, 128 * j : 128 * (j + 1)] = f_v[
                pl.ds(j, 64, stride=16), :
            ].astype(BF)

    lane = lax.broadcasted_iota(jnp.int32, (1, 896), 1)

    def one(pg, carry):
        tok = pl.ds(pg * 256, 256)
        src = xin[pg].reshape(256, 2 * D)
        ghat, _ = normalise(src[:, :D].astype(F32))
        normed = ghat.astype(BF)
        norm_v[tok, :] = normed
        dz = (gate_ref[...] * src[:, D:].astype(F32)).astype(BF)
        dz_v[tok, :] = dz
        qkv = jnp.dot(normed, w_v[:, 0:896], preferred_element_type=F32)
        od = jnp.dot(dz, w_v[:, 768:1152], preferred_element_type=F32)
        qa = qkv[:, 0:384].astype(BF)
        ka = turn(qkv[:, 256:640], -32).astype(BF)
        va = turn(qkv[:, 512:896], -64).astype(BF)
        da = turn(od, -96).astype(BF)
        dq, dk, dv, att = attention(qa, ka, va, da)
        dk, dv, att = turn(dk, 32), turn(dv, 64), turn(att, 96)
        tiles = [[] for _ in range(9)]
        for start, val in ((0, dq), (2, dk), (4, dv), (6, att)):
            for t in range(3):
                tiles[start + t].append(val[:, 128 * t : 128 * (t + 1)])
        for t in range(9):
            g_v[tok, 128 * t : 128 * (t + 1)] = functools.reduce(lambda a, b: a + b, tiles[t]).astype(BF)
        left = jnp.where(lane < 864, g_v[tok, 0:896], jnp.zeros((256, 896), BF))
        dn[pg] = nt(left, w_v[:, 0:896]).astype(BF)
        return carry

    lax.fori_loop(0, 2, one, 0)

    def grads(i):
        c = slice(128 * i, 128 * (i + 1))
        a = tn(norm_v[:, c], g_v[:, 0:896])
        b = tn(dz_v[:, c], g_v[:, 768:1152])
        lane = lax.broadcasted_iota(jnp.int32, (1, 128), 1)
        mid = jnp.where(lane < 96, a[:, 768:896], b[:, 0:128])
        return jnp.concatenate([a[:, 0:768], mid, b[:, 128:384]], 1)

    for i in range(8):
        dw[8 * i : 8 * i + 8, :, 0:D] = grads(i).astype(BF).reshape(8, 16, D)
    rest = grads(8)
    for r in range(2):
        f_v[...] = jnp.zeros((1024, 128), F32)
        for j in range(9):
            f_v[pl.ds(j, 64, stride=16), :] = rest[64 * r : 64 * r + 64, 128 * j : 128 * (j + 1)]
        dw[:, :, D + 128 * r : D + 128 * (r + 1)] = f_v[...].astype(BF).reshape(64, 16, 128)


def scatter_kernel(
    dw, dn, xin, gw, out,
    own_y, ry, py, rx, px, rz, g_v, gs_v, dn_own, rs, ps, rh, xi_v, res_v, og, perm_v,
    y_send, y_recv, x_sem, z_send, z_recv, g_sem, s_sem, h_sem, o_send, o_recv, l_sem,
):
    x, z, y, core, h = place()
    zl = z % 2
    ck = zl * 4 + y
    member = ck * 2 + core
    sibling = (seq_of(x, z, y, 1 - core), h)
    x_peer = (seq_of(1 - x, z, y, core), h)
    h_peer = (seq_of(x, z, y, core), 1 - h)
    z_peers = [(seq_of(x, (z + d) % 8, y, core), h) for d in range(1, 8)]
    y_peers = [(seq_of(x, z, (y + d) % 4, core), h) for d in range(1, 4)]
    base = (x * 8 + (z // 2) * 2) * 8
    group = [(base + (member + i) % 16, (h + k) % 2) for i in range(16) for k in range(2)][1:]
    everyone = [x_peer] + z_peers + group
    barrier = pltpu.get_barrier_semaphore()
    for peer in everyone:
        signal(barrier, peer)
    pl.semaphore_wait(barrier, len(everyone))

    swap = remote(dn.at[1 - core], rs, s_sem.at[0], s_sem.at[1], sibling)
    swap.start()
    y_copies = [
        remote(dw.at[:, :, (y + d) % 4], ry.at[d - 1], y_send.at[d - 1], y_recv.at[d - 1], y_peers[d - 1])
        for d in range(1, 4)
    ]
    for c in y_copies:
        c.start()
    keep = pltpu.make_async_copy(dn.at[core], dn_own, l_sem.at[0])
    keep.start()
    keep_y = pltpu.make_async_copy(dw.at[:, :, y], own_y, l_sem.at[1])
    keep_y.start()
    tokens = pltpu.make_async_copy(xin.at[core, pl.ds(4 * h, 4)], xi_v, l_sem.at[2])
    tokens.start()
    row = lax.broadcasted_iota(jnp.int32, (D, 1), 0)
    perm_v[...] = jnp.where(row == permuted_feature((1, D), 1), 1.0, 0.0).astype(BF)
    keep.wait()
    swap.wait()
    ps[...] = (dn_own[...].astype(F32) + rs[...].astype(F32)).astype(BF)
    half = remote(ps.at[pl.ds((1 - h) * 128, 128)], rh, h_sem.at[0], h_sem.at[1], h_peer)
    half.start()
    tokens.wait()
    src = xi_v[...].reshape(128, 2 * D)
    ghat, rstd = normalise(src[:, :D].astype(F32))
    half.wait()
    mine = ps[pl.ds(pl.multiple_of(h * 128, 128), 128), :].astype(F32) + rh[...].astype(F32)
    mine = mine.astype(BF).astype(F32)
    one = jnp.mean(mine, -1, keepdims=True)
    two = jnp.mean(mine * ghat, -1, keepdims=True)
    res = src[:, D:].astype(F32) + rstd * (mine - one - ghat * two)
    res_v[...] = res.astype(BF).reshape(8, 16, D)
    o_copies = []
    for i in range(8):
        for k in range(2):
            o_copies.append((i, k))

    def send_out(i, k):
        to = lax.rem(member + i, 8)
        target = (base + 8 * h + to, (h + k) % 2)
        return remote(res_v.at[to], og.at[member], o_send.at[2 * i + k], o_recv.at[member], target)

    local = zl == h
    for i, k in o_copies:
        if i == 0 and k == 0:
            @pl.when(jnp.logical_not(local))
            def _():
                send_out(0, 0).start()

            @pl.when(local)
            def _():
                pltpu.make_async_copy(res_v.at[lax.rem(member, 8)], og.at[member], l_sem.at[3]).start()
        else:
            send_out(i, k).start()

    keep_y.wait()
    for c in y_copies:
        c.wait()

    def add_y(xx):
        t = own_y[xx].astype(F32)
        for d in range(3):
            t = t + ry[d, xx].astype(F32)
        py[xx] = t.astype(BF)

    add_y(1 - x)
    x_copy = remote(py.at[1 - x], rx, x_sem.at[0], x_sem.at[1], x_peer)
    x_copy.start()
    add_y(x)
    x_copy.wait()
    px[...] = (py[x].astype(F32) + rx[...].astype(F32)).astype(BF)
    z_copies = [
        remote(px.at[(z + d) % 8], rz.at[d - 1], z_send.at[d - 1], z_recv.at[d - 1], z_peers[d - 1])
        for d in range(1, 8)
    ]
    for c in z_copies:
        c.start()
    for c in z_copies:
        c.wait()
    t = px[z].astype(F32)
    for d in range(7):
        t = t + rz[d].astype(F32)
    g_v[...] = t
    g_copy = remote(g_v, gs_v, g_sem.at[0], g_sem.at[1], sibling)
    g_copy.start()

    for i, k in o_copies:
        if i == 0 and k == 0:
            @pl.when(jnp.logical_not(local))
            def _():
                send_out(0, 0).wait_send()

            @pl.when(local)
            def _():
                pltpu.make_async_copy(res_v.at[lax.rem(member, 8)], og.at[member], l_sem.at[3]).wait()
        else:
            send_out(i, k).wait_send()
    for m in range(16):
        @pl.when(jnp.logical_not(local & (member == m)))
        def _():
            remote(res_v.at[0], og.at[m], o_send.at[0], o_recv.at[m], h_peer).wait_recv()

    back = jnp.dot(og[...].reshape(256, D), perm_v[...], preferred_element_type=F32)
    for f in range(2):
        for g in range(8):
            a = back[32 * g + 8 * f : 32 * g + 8 * f + 8]
            b = back[32 * g + 16 + 8 * f : 32 * g + 24 + 8 * f]
            out[f, 16 * g : 16 * g + 16, :] = jnp.concatenate([a, b], 0).astype(BF)
    g_copy.wait()
    gw[core] = g_v[...]
    gw[1 - core] = gs_v[...]


def on_device(inputs, out_grad, gate, qkv_weight, out_weight):
    core = lax.axis_index("seq") % 2
    vm = pl.BlockSpec(memory_space=pltpu.VMEM)
    hbm = pl.BlockSpec(memory_space=pl.ANY)
    dma = pltpu.SemaphoreType.DMA

    w = jnp.concatenate([qkv_weight, out_weight[:, None]], 1).reshape(9, 4, 2, 288)
    w = w.transpose(2, 0, 1, 3).reshape(2, 9, D)
    main = w[:, :8]
    last = jnp.pad(w[:, 8].reshape(2, 9, 128), ((0, 0), (0, 7), (0, 0)))
    zero = jnp.zeros_like
    main = jnp.where(
        core == 0, jnp.concatenate([main, zero(main)], 1), jnp.concatenate([zero(main), main], 1)
    )
    last = jnp.where(
        core == 0, jnp.concatenate([last, zero(last)], 2), jnp.concatenate([zero(last), last], 2)
    )
    wsh = jnp.concatenate([main, last], 2)

    buf, xin = pl.pallas_call(
        gather_kernel,
        out_shape=[
            jax.ShapeDtypeStruct((XS, ZS, YS, 16, BLK), BF),
            jax.ShapeDtypeStruct((2, 8, 2, 16, 2 * D), BF),
        ],
        in_specs=[vm] * 3,
        out_specs=[hbm, hbm],
        scratch_shapes=[
            pltpu.VMEM((16, BLK), BF), pltpu.VMEM((16, BLK), BF),
            pltpu.VMEM((16, 16, 2 * D), BF), pltpu.VMEM((D, D), BF),
            dma((2,)), dma((7,)), dma((7,)), dma((2,)), dma((6,)), dma((6,)),
            dma((7,)), dma((7,)), dma((2,)), dma((2,)),
        ],
        compiler_params=pltpu.CompilerParams(
            collective_id=0, has_side_effects=True, vmem_limit_bytes=VMEM_BYTES
        ),
        name="gather",
    )(inputs, out_grad, wsh)

    gate_p = jnp.concatenate([gate.reshape(128, 9)[:, :8].reshape(1024), gate.reshape(64, 2, 9)[:, :, 8].T.reshape(128)])
    dw, dn = pl.pallas_call(
        compute_kernel,
        out_shape=[
            jax.ShapeDtypeStruct((CHIPS, 16, BLK), BF),
            jax.ShapeDtypeStruct((2, 256, D), BF),
        ],
        in_specs=[vm] * 3,
        out_specs=[vm, vm],
        scratch_shapes=[
            pltpu.VMEM((D, D), BF), pltpu.VMEM((512, D), BF), pltpu.VMEM((512, D), BF),
            pltpu.VMEM((512, D), BF), pltpu.VMEM((1024, 128), F32),
        ],
        compiler_params=pltpu.CompilerParams(vmem_limit_bytes=VMEM_BYTES),
        name="compute",
    )(buf.reshape(CHIPS, 16, BLK), xin, gate_p.reshape(1, D))

    gw, grad_inputs = pl.pallas_call(
        scatter_kernel,
        out_shape=[
            jax.ShapeDtypeStruct((2, 16, BLK), F32),
            jax.ShapeDtypeStruct((2, 128, D), BF),
        ],
        in_specs=[hbm] * 3,
        out_specs=[vm, vm],
        scratch_shapes=[
            pltpu.VMEM((XS, ZS, 16, BLK), BF), pltpu.VMEM((3, XS, ZS, 16, BLK), BF),
            pltpu.VMEM((XS, ZS, 16, BLK), BF), pltpu.VMEM((ZS, 16, BLK), BF),
            pltpu.VMEM((ZS, 16, BLK), BF), pltpu.VMEM((7, 16, BLK), BF),
            pltpu.VMEM((16, BLK), F32), pltpu.VMEM((16, BLK), F32),
            pltpu.VMEM((256, D), BF), pltpu.VMEM((256, D), BF), pltpu.VMEM((256, D), BF),
            pltpu.VMEM((128, D), BF), pltpu.VMEM((4, 2, 16, 2 * D), BF),
            pltpu.VMEM((8, 16, D), BF), pltpu.VMEM((16, 16, D), BF), pltpu.VMEM((D, D), BF),
            dma((3,)), dma((3,)), dma((2,)), dma((7,)), dma((7,)), dma((2,)), dma((2,)), dma((2,)),
            dma((16,)), dma((16,)), dma((4,)),
        ],
        compiler_params=pltpu.CompilerParams(
            collective_id=1, has_side_effects=True, vmem_limit_bytes=VMEM_BYTES
        ),
        name="scatter",
    )(dw.reshape(XS, ZS, YS, 16, BLK), dn, xin)

    main = jnp.where(core == 0, gw[:, 0:8, :D], gw[:, 8:16, :D])
    last = jnp.where(core == 0, gw[:, 0:9, D : D + 128], gw[:, 0:9, D + 128 :]).reshape(2, 1, D)
    full = jnp.concatenate([main, last], 1).reshape(2, 9, 4, 288).transpose(1, 2, 0, 3)
    full = full.reshape(9, 4, 576)
    return grad_inputs, full[:, 0:3], full[:, 3]


def solution(mesh):
    in_specs = (
        P("seq", None, None),
        P("seq", None, None),
        P(),
        P("seq", None, "head"),
        P("seq", "head"),
    )
    out_specs = (P("seq", None, None), P("seq", None, "head"), P("seq", "head"))
    return jax.shard_map(
        on_device, mesh=mesh, in_specs=in_specs, out_specs=out_specs, check_vma=False
    )
```

time: 1750 us -> 158 us (0.09)
  waiting for transfers between devices: 1590 us -> 0 us
  Pallas kernels: 0 us -> 145 us
  local copies, waits for them, and re-layouts: 61 us -> 7.83 us
  blocking collectives: 46.8 us -> 0 us
  matrix products: 19.5 us -> 0 us
    unnamed x5 -> x0, waiting for transfers between devices: 1300 us -> none
    all_gather x2 -> x0, waiting for transfers between devices: 236 us -> none  [the longest x1 120 us: on_device(): lax.all_gather(out_weight, 'seq', axis=0, tiled=True)]
    pallas_call x0 -> x3, Pallas kernels: none -> 145 us  [the longest x1 63.8 us: on_device(): pl.pallas_call(gather_kernel, out_shape=[jax.ShapeDtypeStruct((XS, ZS, YS...]
    all_to_all x1 -> x0, blocking collectives: 46.8 us -> none  [on_device(): lax.all_to_all(jnp.concatenate([qkv, dout], 2), 'seq', split_axis=1, conc...]
    all_to_all x1 -> x0, waiting for transfers between devices: 36.9 us -> none  [on_device(): back = lax.all_to_all(grads, 'seq', split_axis=0, concat_axis=1, tiled=True)]
    dot_general x10 -> x0, matrix products: 17.9 us -> none  [the longest x1 4.66 us: finish_grads(): lax.dot_general(dqkv, w_flat, (((1,), (1,)), ((), ())), preferred_element...]
  transfers between devices with their start and end apart: 5 -> 0, of which waited for: 5 -> 0; matrix products, arithmetic and copies ran while one was open for 2% -> 0% of each run, Pallas kernels for 0% -> 0%
where the time goes in v1:
time: 158 us; the launch traced here: 156 us
  Pallas kernels  145 us (92%)
  local copies, waits for them, and re-layouts  7.83 us (5%)
  other arithmetic  2.47 us (2%)
    pallas_call x1, Pallas kernels, on_device(): pl.pallas_call(gather_kernel, out_shape=[jax.ShapeDtypeStruct((XS, ZS, YS...  63.8 us
    pallas_call x1, Pallas kernels, on_device(): pl.pallas_call(scatter_kernel, out_shape=[jax.ShapeDtypeStruct((2, 16, BL...  63.3 us
    pallas_call x1, Pallas kernels, on_device(): pl.pallas_call(compute_kernel, out_shape=[jax.ShapeDtypeStruct((CHIPS, 16...  17.5 us

profile of v1, /device:TPU:1, one launch (start us, length us, event | category | flops | bytes accessed | tf_op | source)
XLA Modules:
  0.0 155.7 jit_solution(1045322347201665337)
XLA Ops:
  0.6 0.8 concatenate.46
  1.5 0.9 concatenate.34
  2.4 0.1 maximum_bitcast_fusion.1
  2.5 0.2 reshape.42
  2.8 0.6 pad_maximum_fusion.wsh_ref
  3.4 0.9 reshape.46
  4.4 0.1 slice.43
  4.5 0.1 copy.16
  4.6 0.1 reshape.47
  4.7 0.9 reshape.44
  5.6 0.1 reshape.45
  5.7 0.6 reshape.48.gate_ref
  6.3 63.8 %gather.1 = (bf16[2,8,4,16,1408]{4,3,2,1,0:T(8,128)(2,1)}, bf16[2,8,2,16,2304]{4,3,2,1,0:T(8,128)(2,1)}) custom-call(bf16[2,128,1152]{2,1,0:T(8,128)(2,1)} %in_ref.1, bf16[2,128,1152]{2,1,0:T(8,128)(2,1)} %up_ref.1, bf16[2,16,1408]{2,1,0:T(8,128)(2,1)} %pad_maximum_fusion.wsh_ref), custom_call_target="tpu_custom_call" | custom-call | tf_op jit(solution)/shard_map/gather/pallas_call | solution.py:388
  70.1 17.5 %compute.1 = (bf16[64,16,1408]{2,1,0:T(8,128)(2,1)}, bf16[2,256,1152]{2,1,0:T(8,128)(2,1)}) custom-call(bf16[64,16,1408]{2,1,0:T(8,128)(2,1)} %bitcast.19, bf16[2,8,2,16,2304]{4,3,2,1,0:T(8,128)(2,1)} %get-tuple-element.10.xin, f32[1,1152]{1,0:T(1,128)} %reshape.48.gate_ref), custom_call_target="tpu_custom_call" | custom-call | tf_op jit(solution)/shard_map/compute/pallas_call | solution.py:409
  87.6 63.3 %scatter.1 = (f32[2,16,1408]{2,1,0:T(8,128)}, bf16[2,128,1152]{2,1,0:T(8,128)(2,1)}) custom-call(bf16[2,8,4,16,1408]{4,3,2,1,0:T(8,128)(2,1)} %bitcast.18, bf16[2,256,1152]{2,1,0:T(8,128)(2,1)} %get-tuple-element.12.dn, bf16[2,8,2,16,2304]{4,3,2,1,0:T(8,128)(2,1)} %get-tuple-element.10.xin), custom_call_target="tpu_custom_call" | custom-call | tf_op jit(solution)/shard_map/scatter/pallas_call | solution.py:425
  150.9 0.7 slice_select_fusion.1
  151.7 0.9 slice_select_fusion
  152.6 0.1 concatenate.44
  152.7 0.1 concatenate.43
  152.8 0.1 copy.17
  152.9 0.1 maximum_bitcast_fusion
  153.0 0.1 reshape.50
  153.1 0.0 copy-start
  153.1 0.6 copy.22
  153.8 1.9 %copy.24 = bf16[2,128,1152]{2,1,0:T(8,128)(2,1)} copy(bf16[2,128,1152]{2,1,0:T(8,128)(2,1)} %get-tuple-element.21) | data formatting | bytes 1179648
  155.7 0.0 copy-done
  (11 shorter events, 0.2 us)
Async XLA Ops:
  153.1 2.6 %copy-start = (f32[9,4,576]{2,1,0:T(4,128)}, f32[9,4,576]{2,1,0:T(4,128)S(1)}, u32[]{:S(2)}) copy-start(f32[9,4,576]{2,1,0:T(4,128)S(1)} %reshape.50) | copy-start | bytes 248836

commit v2 on v1

v2 whole, which is shorter than its diff:
```python
import functools

import jax
import jax.numpy as jnp
from jax import lax
from jax.experimental import pallas as pl
from jax.experimental.pallas import tpu as pltpu
from jax.sharding import PartitionSpec as P

D = 1152
HEAD_DIM = 72
XS, ZS, YS = 2, 8, 4
CHIPS = XS * ZS * YS
BLK = 1408
PW = 512
RW = BLK - PW
RM = D - PW
MESH = pl.DeviceIdType.MESH
BF = jnp.bfloat16
F32 = jnp.float32
VMEM_BYTES = 58 * 2**20


def place():
    s = lax.axis_index("seq")
    h = lax.axis_index("head")
    return s // 64, (s // 8) % 8, (s // 2) % 4, s % 2, h


def seq_of(x, z, y, core):
    return ((x * 8 + z) * 4 + y) * 2 + core


def signal(sem, target):
    pl.semaphore_signal(sem, inc=1, device_id=target, device_id_type=MESH)


def remote(src, dst, send, recv, target):
    return pltpu.make_async_remote_copy(
        src_ref=src, dst_ref=dst, send_sem=send, recv_sem=recv, device_id=target, device_id_type=MESH
    )


def permuted_feature(shape, dim):
    f = lax.broadcasted_iota(jnp.int32, shape, dim)
    owner = f // 9
    q = f - owner * 9
    return jnp.where(q < 8, owner * 8 + q, 1024 + (owner % 2) * 64 + owner // 2)


class Copies:
    def __init__(self, send, recv):
        self.send, self.recv, self.count = send, recv, 0

    def start(self, src, dst, target):
        k = self.count
        self.count += 1
        c = remote(src, dst, self.send.at[k], self.recv.at[k], target)
        c.start()
        return c


def gather_kernel(
    in_ref, up_ref, wsh_ref, buf_p, buf_r, xin,
    sib_v, mine_p, mine_r, xg_v, perm_v, send_sem, recv_sem, l_sem,
):
    x, z, y, core, h = place()
    ck = (z % 2) * 4 + y
    up, dn, far = (y + 1) % 4, (y + 3) % 4, (y + 2) % 4
    sibling = (seq_of(x, z, y, 1 - core), h)
    x_peer = (seq_of(1 - x, z, y, core), h)
    h_peer = (seq_of(x, z, y, core), 1 - h)
    y_up = (seq_of(x, z, up, core), h)
    y_dn = (seq_of(x, z, dn, core), h)
    z_peers = [(seq_of(x, (z + d) % 8, y, core), h) for d in range(1, 8)]
    t_chips = [(ck + d) % 8 for d in range(1, 8)]
    t_peers = [(seq_of(x, (z // 2) * 2 + c // 4, c % 4, core), h) for c in t_chips]
    everyone = [sibling, x_peer, h_peer, y_up, y_dn] + z_peers + t_peers
    barrier = pltpu.get_barrier_semaphore()
    for peer in everyone:
        signal(barrier, peer)
    pl.semaphore_wait(barrier, len(everyone))
    net = Copies(send_sem, recv_sem)

    swap = net.start(wsh_ref.at[1 - core], sib_v, sibling)
    swap.wait()
    mine = wsh_ref[core] + sib_v[...]
    mine_p[...] = mine[:, :PW]
    mine_r[...] = mine[:, PW:]
    z_r = [net.start(mine_r, buf_r.at[x, z, y], peer) for peer in z_peers]
    z_p = [net.start(mine_p, buf_p.at[x, z, y], peer) for peer in z_peers]
    own_p = pltpu.make_async_copy(mine_p, buf_p.at[x, z, y], l_sem.at[0])
    own_r = pltpu.make_async_copy(mine_r, buf_r.at[x, z, y], l_sem.at[1])
    own_p.start()
    own_r.start()

    row = permuted_feature((D, 1), 0)
    col = lax.broadcasted_iota(jnp.int32, (1, D), 1)
    perm_v[...] = jnp.where(row == col, 1.0, 0.0).astype(BF)
    for i, ref in enumerate((in_ref, up_ref)):
        p = jnp.dot(ref[...].reshape(256, D), perm_v[...], preferred_element_type=F32)
        for g in range(16):
            part = jnp.concatenate([p[8 * g : 8 * g + 8], p[128 + 8 * g : 136 + 8 * g]], 0)
            xg_v[g, :, i * D : (i + 1) * D] = part.astype(BF)
    tok = [
        net.start(xg_v.at[2 * c + h], xin.at[h, ck, core], peer) for c, peer in zip(t_chips, t_peers)
    ]
    own_t = pltpu.make_async_copy(xg_v.at[2 * ck + h], xin.at[h, ck, core], l_sem.at[2])
    own_t.start()

    own_r.wait()
    for c in z_r:
        c.wait()
    r_up = net.start(buf_r.at[x, :, y], buf_r.at[x, :, y], y_up)
    r_dn = net.start(buf_r.at[x, :, y], buf_r.at[x, :, y], y_dn)
    r_x0 = net.start(buf_r.at[x, :, y], buf_r.at[x, :, y], x_peer)
    own_p.wait()
    for c in z_p:
        c.wait()
    p_x = net.start(buf_p.at[x, :, y], buf_p.at[x, :, y], x_peer)
    p_up = net.start(buf_p.at[x, :, y], buf_p.at[x, :, y], y_up)
    p_dn = net.start(buf_p.at[x, :, y], buf_p.at[x, :, y], y_dn)
    lo, hi = pl.ds(0, 4), pl.ds(4, 4)

    r_up.wait_recv()
    r_f0 = net.start(buf_r.at[x, lo, dn], buf_r.at[x, lo, dn], y_up)
    r_x1 = net.start(buf_r.at[x, :, dn], buf_r.at[x, :, dn], x_peer)
    r_dn.wait_recv()
    r_f1 = net.start(buf_r.at[x, hi, up], buf_r.at[x, hi, up], y_dn)
    r_x2 = net.start(buf_r.at[x, :, up], buf_r.at[x, :, up], x_peer)
    p_up.wait_recv()
    p_f0 = net.start(buf_p.at[x, lo, dn], buf_p.at[x, lo, dn], y_up)
    p_dn.wait_recv()
    p_f1 = net.start(buf_p.at[x, hi, up], buf_p.at[x, hi, up], y_dn)
    p_x.wait_recv()
    q_up = net.start(buf_p.at[1 - x, :, y], buf_p.at[1 - x, :, y], y_up)
    q_dn = net.start(buf_p.at[1 - x, :, y], buf_p.at[1 - x, :, y], y_dn)

    own_t.wait()
    for c in tok:
        c.wait_recv()
    t_h = net.start(xin.at[h, :, core], xin.at[h, :, core], h_peer)
    t_s = net.start(xin.at[h, :, core], xin.at[h, :, core], sibling)

    r_f0.wait_recv()
    r_x3 = net.start(buf_r.at[x, lo, far], buf_r.at[x, lo, far], x_peer)
    r_f1.wait_recv()
    r_x4 = net.start(buf_r.at[x, hi, far], buf_r.at[x, hi, far], x_peer)
    q_up.wait_recv()
    q_f0 = net.start(buf_p.at[1 - x, lo, dn], buf_p.at[1 - x, lo, dn], y_up)
    q_dn.wait_recv()
    q_f1 = net.start(buf_p.at[1 - x, hi, up], buf_p.at[1 - x, hi, up], y_dn)
    t_h.wait_recv()
    t_s2 = net.start(xin.at[1 - h, :, core], xin.at[1 - h, :, core], sibling)
    for c in (p_f0, p_f1, r_x0, r_x1, r_x2, r_x3, r_x4, q_f0, q_f1, t_s, t_s2):
        c.wait()
    for c in [r_up, r_dn, p_x, p_up, p_dn, r_f0, r_f1, q_up, q_dn, t_h] + tok:
        c.wait_send()


def normalise(v):
    mean = jnp.mean(v, -1, keepdims=True)
    centered = v - mean
    rstd = lax.rsqrt(jnp.mean(centered * centered, -1, keepdims=True) + 1e-06)
    return centered * rstd, rstd


def turn(v, by):
    return jnp.concatenate([v[:, -by:], v[:, :-by]], 1)


def nt(a, b):
    return lax.dot_general(a, b, (((1,), (1,)), ((), ())), preferred_element_type=F32)


def tn(a, b):
    return lax.dot_general(a, b, (((0,), (0,)), ((), ())), preferred_element_type=F32)


def attention(qa, ka, va, da):
    scale = HEAD_DIM ** (-0.5)
    rows = lax.broadcasted_iota(jnp.int32, (256, 256), 0)
    cols = lax.broadcasted_iota(jnp.int32, (256, 256), 1)
    same = (rows & 7) == (cols & 7)
    outs = [[[] for _ in range(3)] for _ in range(4)]
    for head, (lo, hi) in enumerate(((0, 128), (0, 256), (128, 256), (128, 384))):
        lane = lax.broadcasted_iota(jnp.int32, (1, hi - lo), 1) + lo
        keep = (lane >= HEAD_DIM * head) & (lane < HEAD_DIM * (head + 1))
        q, k, v, d = (a[:, lo:hi] for a in (qa, ka, va, da))
        qm = jnp.where(keep, q, jnp.zeros_like(q))
        dm = jnp.where(keep, d, jnp.zeros_like(d))
        scores = jnp.where(same, nt(qm, k) * scale, -1e30)
        top = jnp.max(scores, -1, keepdims=True)
        e = jnp.exp(scores - top)
        probs = e / jnp.sum(e, -1, keepdims=True)
        probs_b = probs.astype(BF)
        att = jnp.dot(probs_b, v, preferred_element_type=F32).astype(BF)
        delta = jnp.sum(dm.astype(F32) * att.astype(F32), -1, keepdims=True)
        ds = (probs * (nt(dm, v) - delta) * scale).astype(BF)
        dq = jnp.dot(ds, k, preferred_element_type=F32)
        dk = tn(ds, q)
        dv = tn(probs_b, d)
        for slot, val in zip(outs, (dq, dk, dv, att.astype(F32))):
            val = jnp.where(keep, val, 0.0)
            for t in range(lo // 128, hi // 128):
                slot[t].append(val[:, t * 128 - lo : t * 128 - lo + 128])
    return [jnp.concatenate([functools.reduce(lambda a, b: a + b, t) for t in s], 1) for s in outs]


def compute_kernel(buf_p, buf_r, xin, gate_ref, dw_p, dw_r, dn, w_v, norm_v, dz_v, g_v, f_v):
    w_v[0:1024, 0:PW] = buf_p[...].reshape(1024, PW)
    w_v[0:1024, PW:D] = buf_r[:, :, 0:RM].reshape(1024, RM)
    for r in range(2):
        f_v[...] = buf_r[:, :, RM + 128 * r : RM + 128 * (r + 1)].reshape(1024, 128).astype(F32)
        for j in range(9):
            w_v[1024 + 64 * r : 1088 + 64 * r, 128 * j : 128 * (j + 1)] = f_v[
                pl.ds(j, 64, stride=16), :
            ].astype(BF)

    lane = lax.broadcasted_iota(jnp.int32, (1, 896), 1)

    def one(pg, carry):
        tok = pl.ds(pg * 256, 256)
        src = xin[pg].reshape(256, 2 * D)
        ghat, _ = normalise(src[:, :D].astype(F32))
        normed = ghat.astype(BF)
        norm_v[tok, :] = normed
        dz = (gate_ref[...] * src[:, D:].astype(F32)).astype(BF)
        dz_v[tok, :] = dz
        qkv = jnp.dot(normed, w_v[:, 0:896], preferred_element_type=F32)
        od = jnp.dot(dz, w_v[:, 768:1152], preferred_element_type=F32)
        qa = qkv[:, 0:384].astype(BF)
        ka = turn(qkv[:, 256:640], -32).astype(BF)
        va = turn(qkv[:, 512:896], -64).astype(BF)
        da = turn(od, -96).astype(BF)
        dq, dk, dv, att = attention(qa, ka, va, da)
        dk, dv, att = turn(dk, 32), turn(dv, 64), turn(att, 96)
        tiles = [[] for _ in range(9)]
        for start, val in ((0, dq), (2, dk), (4, dv), (6, att)):
            for t in range(3):
                tiles[start + t].append(val[:, 128 * t : 128 * (t + 1)])
        for t in range(9):
            g_v[tok, 128 * t : 128 * (t + 1)] = functools.reduce(lambda a, b: a + b, tiles[t]).astype(BF)
        left = jnp.where(lane < 864, g_v[tok, 0:896], jnp.zeros((256, 896), BF))
        dn[pg] = nt(left, w_v[:, 0:896]).astype(BF)
        return carry

    lax.fori_loop(0, 2, one, 0)

    def grads(i):
        c = slice(128 * i, 128 * (i + 1))
        a = tn(norm_v[:, c], g_v[:, 0:896])
        b = tn(dz_v[:, c], g_v[:, 768:1152])
        lane = lax.broadcasted_iota(jnp.int32, (1, 128), 1)
        mid = jnp.where(lane < 96, a[:, 768:896], b[:, 0:128])
        return jnp.concatenate([a[:, 0:768], mid, b[:, 128:384]], 1)

    for i in range(8):
        block = grads(i).astype(BF).reshape(8, 16, D)
        dw_p[8 * i : 8 * i + 8] = block[:, :, :PW]
        dw_r[8 * i : 8 * i + 8, :, 0:RM] = block[:, :, PW:]
    rest = grads(8)
    for r in range(2):
        f_v[...] = jnp.zeros((1024, 128), F32)
        for j in range(9):
            f_v[pl.ds(j, 64, stride=16), :] = rest[64 * r : 64 * r + 64, 128 * j : 128 * (j + 1)]
        dw_r[:, :, RM + 128 * r : RM + 128 * (r + 1)] = f_v[...].astype(BF).reshape(64, 16, 128)


def scatter_kernel(
    dw_p, dw_r, dn, xin, gw, out,
    op, ryp, pyp, rxp, pxp, rzp, orr, rxr, pxr, ryr, pyr, rzr,
    g_v, gs_v, dn_own, rs, ps, rh, xi_v, res_v, og, perm_v, send_sem, recv_sem, l_sem,
):
    x, z, y, core, h = place()
    zl = z % 2
    ck = zl * 4 + y
    sibling = (seq_of(x, z, y, 1 - core), h)
    x_peer = (seq_of(1 - x, z, y, core), h)
    h_peer = (seq_of(x, z, y, core), 1 - h)
    z_peers = [(seq_of(x, (z + d) % 8, y, core), h) for d in range(1, 8)]
    y_peers = [(seq_of(x, z, (y + d) % 4, core), h) for d in range(1, 4)]
    base = (x * 8 + (z // 2) * 2) * 8
    member = ck * 2 + core
    group = [(base + (member + i) % 16, h) for i in range(1, 16)]
    everyone = [x_peer, h_peer] + z_peers + group
    barrier = pltpu.get_barrier_semaphore()
    for peer in everyone:
        signal(barrier, peer)
    pl.semaphore_wait(barrier, len(everyone))
    net = Copies(send_sem, recv_sem)

    away = pl.ds(pl.multiple_of((1 - core) * 128, 128), 128)
    here = pl.ds(pl.multiple_of(core * 128, 128), 128)
    swap = net.start(dn.at[:, away], rs, sibling)
    y_p = [net.start(dw_p.at[:, :, (y + d) % 4], ryp.at[d - 1], y_peers[d - 1]) for d in (1, 3, 2)]
    order = (1, 3, 2, 0)
    x_r = {d: net.start(dw_r.at[1 - x, :, (y + d) % 4], rxr.at[d], x_peer) for d in order}
    keep = pltpu.make_async_copy(dn.at[:, here], dn_own, l_sem.at[0])
    keep.start()
    keep_r = pltpu.make_async_copy(dw_r.at[x], orr, l_sem.at[1])
    keep_r.start()
    keep_p = pltpu.make_async_copy(dw_p.at[:, :, y], op, l_sem.at[2])
    keep_p.start()
    tokens = pltpu.make_async_copy(xin.at[h, pl.ds(4 * core, 4)], xi_v, l_sem.at[3])
    tokens.start()
    row = lax.broadcasted_iota(jnp.int32, (D, 1), 0)
    perm_v[...] = jnp.where(row == permuted_feature((1, D), 1), 1.0, 0.0).astype(BF)
    keep.wait()
    swap.wait_recv()
    ps[...] = (dn_own[...].astype(F32) + rs[...].astype(F32)).astype(BF)
    half = net.start(ps.at[1 - h], rh, h_peer)

    keep_r.wait()
    y_r = {}

    def x_sum(d):
        x_r[d].wait_recv()
        pxr[d] = (orr[:, (y + d) % 4].astype(F32) + rxr[d].astype(F32)).astype(BF)
        if d:
            y_r[d] = net.start(pxr.at[d], ryr.at[d - 1], y_peers[d - 1])

    x_sum(1)
    tokens.wait()
    src = xi_v[...].reshape(128, 2 * D)
    ghat, rstd = normalise(src[:, :D].astype(F32))
    half.wait_recv()
    mine = ps[h].astype(F32) + rh[...].astype(F32)
    mine = mine.astype(BF).astype(F32)
    one = jnp.mean(mine, -1, keepdims=True)
    two = jnp.mean(mine * ghat, -1, keepdims=True)
    res = src[:, D:].astype(F32) + rstd * (mine - one - ghat * two)
    res_v[...] = res.astype(BF).reshape(8, 16, D)

    local = zl == core

    def owner(i):
        to = (member + i) % 8
        return remote(
            res_v.at[to], og.at[ck, h], send_sem.at[48 + i], recv_sem.at[48 + ck],
            (base + 8 * core + to, h),
        )

    stay = pltpu.make_async_copy(res_v.at[member % 8], og.at[ck, h], l_sem.at[4])
    pl.when(jnp.logical_not(local))(lambda: owner(0).start())
    pl.when(local)(lambda: stay.start())
    for i in range(1, 8):
        owner(i).start()

    x_sum(3)
    x_sum(2)
    x_sum(0)
    keep_p.wait()
    for c in y_p:
        c.wait_recv()

    def add_y(xx):
        t = op[xx].astype(F32)
        for d in range(3):
            t = t + ryp[d, xx].astype(F32)
        pyp[xx] = t.astype(BF)

    add_y(1 - x)
    x_p = net.start(pyp.at[1 - x], rxp, x_peer)
    add_y(x)
    x_p.wait_recv()
    pxp[...] = (pyp[x].astype(F32) + rxp[...].astype(F32)).astype(BF)
    z_p = [net.start(pxp.at[(z + d) % 8], rzp.at[d - 1], z_peers[d - 1]) for d in range(1, 8)]

    pl.when(jnp.logical_not(local))(lambda: owner(0).wait_send())
    pl.when(local)(lambda: stay.wait())
    for i in range(1, 8):
        owner(i).wait_send()
    for c in range(8):
        got = remote(res_v.at[0], og.at[c, h], send_sem.at[48], recv_sem.at[48 + c], h_peer)
        pl.when(jnp.logical_not(local & (ck == c)))(lambda got=got: got.wait_recv())
    o_h = net.start(og.at[:, h], og.at[:, h], h_peer)

    for d in (1, 3, 2):
        y_r[d].wait_recv()
    t = pxr[0].astype(F32)
    for d in range(3):
        t = t + ryr[d].astype(F32)
    pyr[...] = t.astype(BF)
    z_r = [net.start(pyr.at[(z + d) % 8], rzr.at[d - 1], z_peers[d - 1]) for d in range(1, 8)]

    o_h.wait()
    back = jnp.dot(og[...].reshape(256, D), perm_v[...], preferred_element_type=F32)
    for f in range(2):
        for g in range(8):
            a = back[32 * g + 8 * f : 32 * g + 8 * f + 8]
            b = back[32 * g + 16 + 8 * f : 32 * g + 24 + 8 * f]
            out[f, 16 * g : 16 * g + 16, :] = jnp.concatenate([a, b], 0).astype(BF)

    for part, own, slots, lanes in ((z_p, pxp, rzp, (0, PW)), (z_r, pyr, rzr, (PW, BLK))):
        for c in part:
            c.wait_recv()
        t = own[z].astype(F32)
        for d in range(7):
            t = t + slots[d].astype(F32)
        g_v[:, lanes[0] : lanes[1]] = t
    last = net.start(g_v, gs_v, sibling)
    last.wait()
    gw[core] = g_v[...]
    gw[1 - core] = gs_v[...]
    for c in [swap, half, x_p] + y_p + list(x_r.values()) + list(y_r.values()) + z_p + z_r:
        c.wait_send()


def on_device(inputs, out_grad, gate, qkv_weight, out_weight):
    core = lax.axis_index("seq") % 2
    vm = pl.BlockSpec(memory_space=pltpu.VMEM)
    hbm = pl.BlockSpec(memory_space=pl.ANY)
    dma = pltpu.SemaphoreType.DMA

    w = jnp.concatenate([qkv_weight, out_weight[:, None]], 1).reshape(9, 4, 2, 288)
    w = w.transpose(2, 0, 1, 3).reshape(2, 9, D)
    main = w[:, :8]
    last = jnp.pad(w[:, 8].reshape(2, 9, 128), ((0, 0), (0, 7), (0, 0)))
    zero = jnp.zeros_like
    main = jnp.where(
        core == 0, jnp.concatenate([main, zero(main)], 1), jnp.concatenate([zero(main), main], 1)
    )
    last = jnp.where(
        core == 0, jnp.concatenate([last, zero(last)], 2), jnp.concatenate([zero(last), last], 2)
    )
    wsh = jnp.concatenate([main, last], 2)

    shape = jax.ShapeDtypeStruct
    buf_p, buf_r, xin = pl.pallas_call(
        gather_kernel,
        out_shape=[
            shape((XS, ZS, YS, 16, PW), BF), shape((XS, ZS, YS, 16, RW), BF),
            shape((2, 8, 2, 16, 2 * D), BF),
        ],
        in_specs=[vm] * 3,
        out_specs=[hbm] * 3,
        scratch_shapes=[
            pltpu.VMEM((16, BLK), BF), pltpu.VMEM((16, PW), BF), pltpu.VMEM((16, RW), BF),
            pltpu.VMEM((16, 16, 2 * D), BF), pltpu.VMEM((D, D), BF),
            dma((48,)), dma((48,)), dma((3,)),
        ],
        compiler_params=pltpu.CompilerParams(
            collective_id=0, has_side_effects=True, vmem_limit_bytes=VMEM_BYTES
        ),
        name="gather",
    )(inputs, out_grad, wsh)

    gate_p = jnp.concatenate(
        [gate.reshape(128, 9)[:, :8].reshape(1024), gate.reshape(64, 2, 9)[:, :, 8].T.reshape(128)]
    )
    dw_p, dw_r, dn = pl.pallas_call(
        compute_kernel,
        out_shape=[shape((CHIPS, 16, PW), BF), shape((CHIPS, 16, RW), BF), shape((2, 256, D), BF)],
        in_specs=[vm] * 4,
        out_specs=[vm] * 3,
        scratch_shapes=[
            pltpu.VMEM((D, D), BF), pltpu.VMEM((512, D), BF), pltpu.VMEM((512, D), BF),
            pltpu.VMEM((512, D), BF), pltpu.VMEM((1024, 128), F32),
        ],
        compiler_params=pltpu.CompilerParams(vmem_limit_bytes=VMEM_BYTES),
        name="compute",
    )(buf_p.reshape(CHIPS, 16, PW), buf_r.reshape(CHIPS, 16, RW), xin, gate_p.reshape(1, D))

    bf = lambda *dims: pltpu.VMEM(dims, BF)
    gw, grad_inputs = pl.pallas_call(
        scatter_kernel,
        out_shape=[shape((2, 16, BLK), F32), shape((2, 128, D), BF)],
        in_specs=[hbm] * 4,
        out_specs=[vm, vm],
        scratch_shapes=[
            bf(XS, ZS, 16, PW), bf(3, XS, ZS, 16, PW), bf(XS, ZS, 16, PW),
            bf(ZS, 16, PW), bf(ZS, 16, PW), bf(7, 16, PW),
            bf(ZS, YS, 16, RW), bf(YS, ZS, 16, RW), bf(YS, ZS, 16, RW),
            bf(3, ZS, 16, RW), bf(ZS, 16, RW), bf(7, 16, RW),
            pltpu.VMEM((16, BLK), F32), pltpu.VMEM((16, BLK), F32),
            bf(2, 128, D), bf(2, 128, D), bf(2, 128, D), bf(128, D), bf(4, 2, 16, 2 * D),
            bf(8, 16, D), bf(8, 2, 16, D), bf(D, D),
            dma((56,)), dma((56,)), dma((5,)),
        ],
        compiler_params=pltpu.CompilerParams(
            collective_id=1, has_side_effects=True, vmem_limit_bytes=VMEM_BYTES
        ),
        name="scatter",
    )(dw_p.reshape(XS, ZS, YS, 16, PW), dw_r.reshape(XS, ZS, YS, 16, RW), dn, xin)

    main = jnp.where(core == 0, gw[:, 0:8, :D], gw[:, 8:16, :D])
    last = jnp.where(core == 0, gw[:, 0:9, D : D + 128], gw[:, 0:9, D + 128 :]).reshape(2, 1, D)
    full = jnp.concatenate([main, last], 1).reshape(2, 9, 4, 288).transpose(1, 2, 0, 3)
    full = full.reshape(9, 4, 576)
    return grad_inputs, full[:, 0:3], full[:, 3]


def solution(mesh):
    in_specs = (
        P("seq", None, None),
        P("seq", None, None),
        P(),
        P("seq", None, "head"),
        P("seq", "head"),
    )
    out_specs = (P("seq", None, None), P("seq", None, "head"), P("seq", "head"))
    return jax.shard_map(
        on_device, mesh=mesh, in_specs=in_specs, out_specs=out_specs, check_vma=False
    )
```

time: 158 us -> 145 us (0.918)
  Pallas kernels: 145 us -> 131 us
    pallas_call x3, Pallas kernels: 145 us -> 131 us  [the longest x1 59.1 us: on_device(): pl.pallas_call(gather_kernel, out_shape=[shape((XS, ZS, YS, 16, PW), BF),...]
where the time goes in v2:
time: 145 us; the launch traced here: 142 us
  Pallas kernels  131 us (90%)
  local copies, waits for them, and re-layouts  7.83 us (5%)
  other arithmetic  2.47 us (2%)
    pallas_call x1, Pallas kernels, on_device(): pl.pallas_call(gather_kernel, out_shape=[shape((XS, ZS, YS, 16, PW), BF),...  59.1 us
    pallas_call x1, Pallas kernels, on_device(): pl.pallas_call(scatter_kernel, out_shape=[shape((2, 16, BLK), F32), shape...  54.1 us
    pallas_call x1, Pallas kernels, on_device(): pl.pallas_call(compute_kernel, out_shape=[shape((CHIPS, 16, PW), BF), sha...  17.7 us

profile of v2, /device:TPU:1, one launch (start us, length us, event | category | flops | bytes accessed | tf_op | source)
XLA Modules:
  0.0 141.9 jit_solution(16516727777523477219)
XLA Ops:
  0.6 0.8 concatenate.46
  1.5 0.9 concatenate.34
  2.4 0.1 maximum_bitcast_fusion.1
  2.5 0.2 reshape.48
  2.8 0.6 pad_maximum_fusion.wsh_ref
  3.4 0.9 reshape.53
  4.4 0.1 slice.43
  4.5 0.1 copy.16
  4.6 0.1 reshape.54
  4.7 0.9 reshape.51
  5.6 0.1 reshape.52
  5.7 0.6 reshape.55.gate_ref
  6.3 59.1 %gather.1 = (bf16[2,8,4,16,512]{4,3,2,1,0:T(8,128)(2,1)}, bf16[2,8,4,16,896]{4,3,2,1,0:T(8,128)(2,1)}, bf16[2,8,2,16,2304]{4,3,2,1,0:T(8,128)(2,1)}) custom-call(bf16[2,128,1152]{2,1,0:T(8,128)(2,1)} %in_ref.1, bf16[2,128,1152]{2,1,0:T(8,128)(2,1)} %up_ref.1, bf16[2,16,1408]{2,1,0:T(8,128)(2,1)} %pad_maximum_fusion.wsh_ref), custom_call_target="tpu_custom_call" | custom-call | tf_op jit(solution)/shard_map/gather/pallas_call | solution.py:430
  65.4 17.7 %compute.1 = (bf16[64,16,512]{2,1,0:T(8,128)(2,1)}, bf16[64,16,896]{2,1,0:T(8,128)(2,1)}, bf16[2,256,1152]{2,1,0:T(8,128)(2,1)}) custom-call(bf16[64,16,512]{2,1,0:T(8,128)(2,1)} %bitcast.23, bf16[64,16,896]{2,1,0:T(8,128)(2,1)} %bitcast.21, bf16[2,8,2,16,2304]{4,3,2,1,0:T(8,128)(2,1)} %get-tuple-element.13.xin, f32[1,1152]{1,0:T(1,128)} %reshape.55.gate_ref), custom_call_target="tpu_custom_call" | custom-call | tf_op jit(solution)/shard_map/compute/pallas_call | solution.py:452
  83.1 54.1 %scatter.1 = (f32[2,16,1408]{2,1,0:T(8,128)}, bf16[2,128,1152]{2,1,0:T(8,128)(2,1)}) custom-call(bf16[2,8,4,16,512]{4,3,2,1,0:T(8,128)(2,1)} %bitcast.22, bf16[2,8,4,16,896]{4,3,2,1,0:T(8,128)(2,1)} %bitcast.20, bf16[2,256,1152]{2,1,0:T(8,128)(2,1)} %get-tuple-element.16.dn, bf16[2,8,2,16,2304]{4,3,2,1,0:T(8,128)(2,1)} %get-tuple-element.13.xin), custom_call_target="tpu_custom_call" | custom-call | tf_op jit(solution)/shard_map/scatter/pallas_call | solution.py:466
  137.2 0.7 slice_select_fusion.1
  137.9 0.9 slice_select_fusion
  138.8 0.1 concatenate.44
  138.9 0.1 concatenate.43
  139.0 0.1 copy.17
  139.1 0.1 maximum_bitcast_fusion
  139.2 0.1 reshape.58
  139.3 0.0 copy-start
  139.4 0.6 copy.22
  140.0 1.9 %copy.24 = bf16[2,128,1152]{2,1,0:T(8,128)(2,1)} copy(bf16[2,128,1152]{2,1,0:T(8,128)(2,1)} %get-tuple-element.25) | data formatting | bytes 1179648
  141.9 0.0 copy-done
  (11 shorter events, 0.2 us)
Async XLA Ops:
  139.3 2.6 %copy-start = (f32[9,4,576]{2,1,0:T(4,128)}, f32[9,4,576]{2,1,0:T(4,128)S(1)}, u32[]{:S(2)}) copy-start(f32[9,4,576]{2,1,0:T(4,128)S(1)} %reshape.58) | copy-start | bytes 248836

commit v3 on v0

v3 whole, which is shorter than its diff:
```python
import functools

import jax
import jax.numpy as jnp
from jax import lax
from jax.experimental import pallas as pl
from jax.experimental.pallas import tpu as pltpu
from jax.sharding import PartitionSpec as P

D = 1152
HEAD_DIM = 72
XS, ZS, YS = 2, 8, 4
CHIPS = XS * ZS * YS
BLK = 1408
PW = 896
RW = BLK - PW
RM = D - PW
MESH = pl.DeviceIdType.MESH
BF = jnp.bfloat16
F32 = jnp.float32
VMEM_BYTES = 58 * 2**20


def place():
    s = lax.axis_index("seq")
    h = lax.axis_index("head")
    return s // 64, (s // 8) % 8, (s // 2) % 4, s % 2, h


def seq_of(x, z, y, core):
    return ((x * 8 + z) * 4 + y) * 2 + core


def signal(sem, target):
    pl.semaphore_signal(sem, inc=1, device_id=target, device_id_type=MESH)


def remote(src, dst, send, recv, target):
    return pltpu.make_async_remote_copy(
        src_ref=src, dst_ref=dst, send_sem=send, recv_sem=recv, device_id=target, device_id_type=MESH
    )


def permuted_feature(shape, dim):
    f = lax.broadcasted_iota(jnp.int32, shape, dim)
    owner = f // 9
    q = f - owner * 9
    return jnp.where(q < 8, owner * 8 + q, 1024 + (owner % 2) * 64 + owner // 2)


class Copies:
    def __init__(self, send, recv):
        self.send, self.recv, self.count = send, recv, 0

    def start(self, src, dst, target):
        k = self.count
        self.count += 1
        c = remote(src, dst, self.send.at[k], self.recv.at[k], target)
        c.start()
        return c


class RowSum:
    def __init__(self, net, src, far, got, both, up, down):
        self.net, self.src, self.far, self.got, self.both = net, src, far, got, both
        self.up, self.down = up, down

    def first(self):
        net, src = self.net, self.src
        self.f = [net.start(src(2, LO), self.far.at[0], self.up), net.start(src(2, HI), self.far.at[1], self.down)]
        self.d = [
            net.start(src(1, HI), self.got.at[0, HI], self.up),
            net.start(src(3, LO), self.got.at[1, LO], self.down),
        ]

    def second(self):
        for i, d, half, to in ((0, 1, LO, self.up), (1, 3, HI, self.down)):
            self.f[i].wait_recv()
            t = self.src(d, half)[...].astype(F32) + self.far[i].astype(F32)
            self.both[i] = t.astype(BF)
            self.d.append(self.net.start(self.both.at[i], self.got.at[i, half], to))

    def total(self):
        for c in self.d:
            c.wait_recv()
        t = self.src(0, pl.ds(0, 8))[...].astype(F32)
        return t + self.got[0].astype(F32) + self.got[1].astype(F32)

    def end(self):
        for c in self.f + self.d:
            c.wait_send()


LO, HI = pl.ds(0, 4), pl.ds(4, 4)


def normalise(v):
    mean = jnp.mean(v, -1, keepdims=True)
    centered = v - mean
    rstd = lax.rsqrt(jnp.mean(centered * centered, -1, keepdims=True) + 1e-06)
    return centered * rstd, rstd


def turn(v, by):
    return jnp.concatenate([v[:, -by:], v[:, :-by]], 1)


def nt(a, b):
    return lax.dot_general(a, b, (((1,), (1,)), ((), ())), preferred_element_type=F32)


def tn(a, b):
    return lax.dot_general(a, b, (((0,), (0,)), ((), ())), preferred_element_type=F32)


def attention(qa, ka, va, da):
    scale = HEAD_DIM ** (-0.5)
    rows = lax.broadcasted_iota(jnp.int32, (256, 256), 0)
    cols = lax.broadcasted_iota(jnp.int32, (256, 256), 1)
    same = (rows & 7) == (cols & 7)
    outs = [[[] for _ in range(3)] for _ in range(4)]
    for head, (lo, hi) in enumerate(((0, 128), (0, 256), (128, 256), (128, 384))):
        lane = lax.broadcasted_iota(jnp.int32, (1, hi - lo), 1) + lo
        keep = (lane >= HEAD_DIM * head) & (lane < HEAD_DIM * (head + 1))
        q, k, v, d = (a[:, lo:hi] for a in (qa, ka, va, da))
        qm = jnp.where(keep, q, jnp.zeros_like(q))
        dm = jnp.where(keep, d, jnp.zeros_like(d))
        scores = jnp.where(same, nt(qm, k) * scale, -1e30)
        top = jnp.max(scores, -1, keepdims=True)
        e = jnp.exp(scores - top)
        probs = e / jnp.sum(e, -1, keepdims=True)
        probs_b = probs.astype(BF)
        att = jnp.dot(probs_b, v, preferred_element_type=F32).astype(BF)
        delta = jnp.sum(dm.astype(F32) * att.astype(F32), -1, keepdims=True)
        ds = (probs * (nt(dm, v) - delta) * scale).astype(BF)
        dq = jnp.dot(ds, k, preferred_element_type=F32)
        dk = tn(ds, q)
        dv = tn(probs_b, d)
        for slot, val in zip(outs, (dq, dk, dv, att.astype(F32))):
            val = jnp.where(keep, val, 0.0)
            for t in range(lo // 128, hi // 128):
                slot[t].append(val[:, t * 128 - lo : t * 128 - lo + 128])
    return [jnp.concatenate([functools.reduce(lambda a, b: a + b, t) for t in s], 1) for s in outs]


def kernel(
    in_ref, up_ref, gate_ref, wq_ref, wo_ref, out, gq, go,
    sib_v, away_v, mine_p, mine_r, nat_v, xg_v, perm_v, rstd_v, buf_p, buf_r, xin,
    w_v, g_v, f_v, dw_p, dw_r, dn, rs, ps, rh, res_v, og,
    far_p, got_p, both_p, pyp, rxp, pxp, rzp, rxr, pxr, far_r, got_r, both_r, pyr, rzr, fin_v, fsib_v,
    send_sem, recv_sem, o_send, o_recv, s_send, s_recv, l_sem,
):
    x, z, y, core, h = place()
    zl = z % 2
    ck = zl * 4 + y
    member = ck * 2 + core
    base = (x * 8 + (z // 2) * 2) * 8
    above, below, far = (y + 1) % 4, (y + 3) % 4, (y + 2) % 4
    sibling = (seq_of(x, z, y, 1 - core), h)
    x_peer = (seq_of(1 - x, z, y, core), h)
    h_peer = (seq_of(x, z, y, core), 1 - h)
    y_up = (seq_of(x, z, above, core), h)
    y_dn = (seq_of(x, z, below, core), h)
    z_peers = [(seq_of(x, (z + d) % 8, y, core), h) for d in range(1, 8)]
    t_chips = [(ck + d) % 8 for d in range(1, 8)]
    t_peers = [(seq_of(x, (z // 2) * 2 + c // 4, c % 4, core), h) for c in t_chips]
    group = [(base + (member + i) % 16, h) for i in range(1, 16)]
    everyone = [x_peer, h_peer] + z_peers + group
    barrier = pltpu.get_barrier_semaphore()
    for peer in everyone:
        signal(barrier, peer)

    wq, wo = wq_ref[...].astype(F32), wo_ref[...].astype(F32)
    blocks = []
    for half in range(2):
        c = slice(288 * half, 288 * half + 288)
        rows = jnp.concatenate([wq[:, 0, c], wq[:, 1, c], wq[:, 2, c], wo[:, c]], 1)
        main, last = rows[0:8], rows[8:9]
        last = [last[:, 128 * j : 128 * j + 128] for j in range(9)] + [jnp.zeros((7, 128), F32)]
        last = jnp.concatenate(last, 0)
        main0 = jnp.concatenate([main, jnp.zeros((8, D), F32)], 0)
        main1 = jnp.concatenate([jnp.zeros((8, D), F32), main], 0)
        none = jnp.zeros((16, 128), F32)
        block0 = jnp.concatenate([main0, last, none], 1)
        block1 = jnp.concatenate([main1, none, last], 1)
        blocks.append(jnp.where(core == 0, block0, block1))
    away_v[...] = jnp.where(core == 0, blocks[1], blocks[0]).astype(BF)
    mine = jnp.where(core == 0, blocks[0], blocks[1])
    pl.semaphore_wait(barrier, len(everyone))
    net = Copies(send_sem, recv_sem)

    swap = net.start(away_v, sib_v, sibling)
    row = permuted_feature((D, 1), 0)
    col = lax.broadcasted_iota(jnp.int32, (1, D), 1)
    perm_v[...] = jnp.where(row == col, 1.0, 0.0).astype(BF)
    swap.wait()
    mine = (mine + sib_v[...].astype(F32)).astype(BF)
    mine_p[...] = mine[:, :PW]
    mine_r[...] = mine[:, PW:]
    z_r = [net.start(mine_r, buf_r.at[x, z, y], peer) for peer in z_peers]
    z_p = [net.start(mine_p, buf_p.at[x, z, y], peer) for peer in z_peers]
    buf_p[x, z, y] = mine[:, :PW]
    buf_r[x, z, y] = mine[:, PW:]

    ghat, rstd = normalise(in_ref[...].reshape(256, D).astype(F32))
    rstd_v[...] = rstd
    dz = gate_ref[...] * up_ref[...].reshape(256, D).astype(F32)
    for i, val in enumerate((ghat, dz)):
        nat_v[...] = val.astype(BF)
        p = jnp.dot(nat_v[...], perm_v[...], preferred_element_type=F32)
        for g in range(16):
            part = jnp.concatenate([p[8 * g : 8 * g + 8], p[128 + 8 * g : 136 + 8 * g]], 0)
            xg_v[g, :, i * D : (i + 1) * D] = part.astype(BF)
    tok = [
        net.start(xg_v.at[2 * c + h], xin.at[h, ck, core], peer) for c, peer in zip(t_chips, t_peers)
    ]
    own_t = pltpu.make_async_copy(xg_v.at[2 * ck + h], xin.at[h, ck, core], l_sem.at[0])
    own_t.start()

    for c in z_r:
        c.wait()
    r_up = net.start(buf_r.at[x, :, y], buf_r.at[x, :, y], y_up)
    r_dn = net.start(buf_r.at[x, :, y], buf_r.at[x, :, y], y_dn)
    r_x0 = net.start(buf_r.at[x, :, y], buf_r.at[x, :, y], x_peer)
    for c in z_p:
        c.wait()
    p_x = net.start(buf_p.at[x, :, y], buf_p.at[x, :, y], x_peer)
    p_up = net.start(buf_p.at[x, :, y], buf_p.at[x, :, y], y_up)
    p_dn = net.start(buf_p.at[x, :, y], buf_p.at[x, :, y], y_dn)

    r_up.wait_recv()
    r_f0 = net.start(buf_r.at[x, LO, below], buf_r.at[x, LO, below], y_up)
    r_x1 = net.start(buf_r.at[x, :, below], buf_r.at[x, :, below], x_peer)
    r_dn.wait_recv()
    r_f1 = net.start(buf_r.at[x, HI, above], buf_r.at[x, HI, above], y_dn)
    r_x2 = net.start(buf_r.at[x, :, above], buf_r.at[x, :, above], x_peer)
    p_up.wait_recv()
    p_f0 = net.start(buf_p.at[x, LO, below], buf_p.at[x, LO, below], y_up)
    p_dn.wait_recv()
    p_f1 = net.start(buf_p.at[x, HI, above], buf_p.at[x, HI, above], y_dn)
    p_x.wait_recv()
    q_up = net.start(buf_p.at[1 - x, :, y], buf_p.at[1 - x, :, y], y_up)
    q_dn = net.start(buf_p.at[1 - x, :, y], buf_p.at[1 - x, :, y], y_dn)

    own_t.wait()
    for c in tok:
        c.wait_recv()
    t_h = net.start(xin.at[h, :, core], xin.at[h, :, core], h_peer)
    t_s = net.start(xin.at[h, :, core], xin.at[h, :, core], sibling)

    r_f0.wait_recv()
    r_x3 = net.start(buf_r.at[x, LO, far], buf_r.at[x, LO, far], x_peer)
    r_f1.wait_recv()
    r_x4 = net.start(buf_r.at[x, HI, far], buf_r.at[x, HI, far], x_peer)
    q_up.wait_recv()
    q_f0 = net.start(buf_p.at[1 - x, LO, below], buf_p.at[1 - x, LO, below], y_up)
    q_dn.wait_recv()
    q_f1 = net.start(buf_p.at[1 - x, HI, above], buf_p.at[1 - x, HI, above], y_dn)
    t_h.wait_recv()
    t_s2 = net.start(xin.at[1 - h, :, core], xin.at[1 - h, :, core], sibling)
    for c in (p_f0, p_f1, r_x0, r_x1, r_x2, r_x3, r_x4, q_f0, q_f1, t_s, t_s2):
        c.wait()
    for c in [r_up, r_dn, p_x, p_up, p_dn, r_f0, r_f1, q_up, q_dn, t_h] + tok:
        c.wait_send()

    w_v[0:1024, 0:PW] = buf_p[...].reshape(1024, PW)
    w_v[0:1024, PW:D] = buf_r[:, :, :, :, 0:RM].reshape(1024, RM)
    for r in range(2):
        f_v[...] = buf_r[:, :, :, :, RM + 128 * r : RM + 128 * (r + 1)].reshape(1024, 128).astype(F32)
        for j in range(9):
            w_v[1024 + 64 * r : 1088 + 64 * r, 128 * j : 128 * (j + 1)] = f_v[
                pl.ds(j, 64, stride=16), :
            ].astype(BF)

    lane = lax.broadcasted_iota(jnp.int32, (1, 896), 1)
    away = pl.ds(pl.multiple_of((1 - core) * 128, 128), 128)
    here = pl.ds(pl.multiple_of(core * 128, 128), 128)

    def swap_dn(pg):
        return remote(dn.at[pg, away], rs.at[pg], s_send.at[pg], s_recv.at[pg], sibling)

    def tokens(pg, carry):
        tok = pl.ds(pg * 256, 256)
        src = xin[pg].reshape(256, 2 * D)
        qkv = jnp.dot(src[:, :D], w_v[:, 0:896], preferred_element_type=F32)
        od = jnp.dot(src[:, D:], w_v[:, 768:1152], preferred_element_type=F32)
        qa = qkv[:, 0:384].astype(BF)
        ka = turn(qkv[:, 256:640], -32).astype(BF)
        va = turn(qkv[:, 512:896], -64).astype(BF)
        da = turn(od, -96).astype(BF)
        dq, dk, dv, att = attention(qa, ka, va, da)
        dk, dv, att = turn(dk, 32), turn(dv, 64), turn(att, 96)
        tiles = [[] for _ in range(9)]
        for start, val in ((0, dq), (2, dk), (4, dv), (6, att)):
            for t in range(3):
                tiles[start + t].append(val[:, 128 * t : 128 * (t + 1)])
        for t in range(9):
            g_v[tok, 128 * t : 128 * (t + 1)] = functools.reduce(lambda a, b: a + b, tiles[t]).astype(BF)
        left = jnp.where(lane < 864, g_v[tok, 0:896], jnp.zeros((256, 896), BF))
        dn[pg] = nt(left, w_v[:, 0:896]).astype(BF)
        swap_dn(pg).start()
        return carry

    lax.fori_loop(0, 2, tokens, 0)

    def grads(i):
        a = tn(xin[:, :, :, :, pl.ds(pl.multiple_of(128 * i, 128), 128)].reshape(512, 128), g_v[:, 0:896])
        b = tn(
            xin[:, :, :, :, pl.ds(pl.multiple_of(D + 128 * i, 128), 128)].reshape(512, 128),
            g_v[:, 768:1152],
        )
        lane = lax.broadcasted_iota(jnp.int32, (1, 128), 1)
        mid = jnp.where(lane < 96, a[:, 768:896], b[:, 0:128])
        return jnp.concatenate([a[:, 0:768], mid, b[:, 128:384]], 1)

    def grad_rows(xx):
        def body(j, carry):
            block = grads(4 * xx + j).astype(BF).reshape(2, 4, 16, D)
            dw_p[xx, pl.ds(2 * j, 2)] = block[:, :, :, :PW]
            dw_r[xx, pl.ds(2 * j, 2), :, :, 0:RM] = block[:, :, :, PW:]
            return carry

        lax.fori_loop(0, 4, body, 0)

    rest = grads(8)
    for r in range(2):
        f_v[...] = jnp.zeros((1024, 128), F32)
        for j in range(9):
            f_v[pl.ds(j, 64, stride=16), :] = rest[64 * r : 64 * r + 64, 128 * j : 128 * (j + 1)]
        dw_r[:, :, :, :, RM + 128 * r : RM + 128 * (r + 1)] = f_v[...].astype(BF).reshape(2, 8, 4, 16, 128)
    grad_rows(1 - x)

    x_r = {d: net.start(dw_r.at[1 - x, :, (y + d) % 4], rxr.at[d], x_peer) for d in (2, 1, 3, 0)}
    sums = [
        RowSum(
            net, (lambda d, zs, xx=xx: dw_p.at[xx, zs, (y + d) % 4]),
            far_p.at[i], got_p.at[i], both_p.at[i], y_up, y_dn,
        )
        for i, xx in enumerate((1 - x, x))
    ]
    sum_r = RowSum(net, (lambda d, zs: pxr.at[d, zs]), far_r, got_r, both_r, y_up, y_dn)
    sums[0].first()
    for pg in range(2):
        swap_dn(pg).wait_recv()
    ps[...] = (dn[:, here].astype(F32) + rs[...].astype(F32)).astype(BF)
    dn_h = net.start(ps.at[1 - h], rh, h_peer)
    grad_rows(x)
    sums[1].first()
    sums[0].second()

    def x_sum(d):
        x_r[d].wait_recv()
        pxr[d] = (dw_r[x, :, (y + d) % 4].astype(F32) + rxr[d].astype(F32)).astype(BF)

    x_sum(2)
    x_sum(1)
    x_sum(3)
    sum_r.first()
    sums[1].second()

    dn_h.wait_recv()
    mine = ps[h].astype(F32) + rh[...].astype(F32)
    mine = mine.astype(BF).astype(F32)
    ghat = xin[h, pl.ds(4 * core, 4), :, :, 0:D].reshape(128, D).astype(F32)
    one = jnp.mean(mine, -1, keepdims=True)
    two = jnp.mean(mine * ghat, -1, keepdims=True)
    res_v[...] = (mine - one - ghat * two).astype(BF).reshape(8, 16, D)

    local = zl == core

    def owner(i):
        to = (member + i) % 8
        target = (base + 8 * core + to, h)
        return remote(res_v.at[to], og.at[ck, h], o_send.at[i], o_recv.at[ck], target)

    stay = pltpu.make_async_copy(res_v.at[member % 8], og.at[ck, h], l_sem.at[1])
    pl.when(jnp.logical_not(local))(lambda: owner(0).start())
    pl.when(local)(lambda: stay.start())
    for i in range(1, 8):
        owner(i).start()

    x_sum(0)
    pyp[0] = sums[0].total().astype(BF)
    x_p = net.start(pyp.at[0], rxp, x_peer)
    sum_r.second()
    pyp[1] = sums[1].total().astype(BF)
    x_p.wait_recv()
    pxp[...] = (pyp[1].astype(F32) + rxp[...].astype(F32)).astype(BF)
    z_p = [net.start(pxp.at[(z + d) % 8], rzp.at[d - 1], z_peers[d - 1]) for d in range(1, 8)]

    pl.when(jnp.logical_not(local))(lambda: owner(0).wait_send())
    pl.when(local)(lambda: stay.wait())
    for i in range(1, 8):
        owner(i).wait_send()
    for c in range(8):
        got = remote(res_v.at[0], og.at[c, h], o_send.at[0], o_recv.at[c], h_peer)
        pl.when(jnp.logical_not(local & (ck == c)))(lambda got=got: got.wait_recv())
    o_h = net.start(og.at[:, h], og.at[:, h], h_peer)

    pyr[...] = sum_r.total().astype(BF)
    z_r = [net.start(pyr.at[(z + d) % 8], rzr.at[d - 1], z_peers[d - 1]) for d in range(1, 8)]

    o_h.wait()
    back = nt(og[...].reshape(256, D), perm_v[...])
    for f in range(2):
        nat = jnp.concatenate([back[16 * g + 8 * f : 16 * g + 8 * f + 8] for g in range(16)], 0)
        nat = up_ref[f].astype(F32) + rstd_v[128 * f : 128 * f + 128] * nat
        out[f] = nat.astype(BF)

    for part, own, slots, lanes in ((z_p, pxp, rzp, (0, PW)), (z_r, pyr, rzr, (PW, BLK))):
        for c in part:
            c.wait_recv()
        t = own[z].astype(F32)
        for d in range(7):
            t = t + slots[d].astype(F32)
        fin_v[:, lanes[0] : lanes[1]] = t
    last = net.start(fin_v, fsib_v, sibling)
    last.wait()

    mine, other = fin_v[...], fsib_v[...]
    rows = []
    for half in (jnp.where(core == 0, mine, other), jnp.where(core == 0, other, mine)):
        main = jnp.where(core == 0, half[0:8, :D], half[8:16, :D])
        tail = jnp.where(core == 0, half[0:9, D : D + 128], half[0:9, D + 128 :])
        tail = jnp.concatenate([tail[j : j + 1] for j in range(9)], 1)
        rows.append(jnp.concatenate([main, tail], 0))
    for t in range(4):
        both = jnp.concatenate([r[:, 288 * t : 288 * t + 288] for r in rows], 1)
        if t < 3:
            gq[:, t, :] = both
        else:
            go[...] = both

    for pg in range(2):
        swap_dn(pg).wait_send()
    for c in [dn_h, x_p] + list(x_r.values()) + z_p + z_r:
        c.wait_send()
    for s in sums + [sum_r]:
        s.end()


def on_device(inputs, out_grad, gate, qkv_weight, out_weight):
    vm = pl.BlockSpec(memory_space=pltpu.VMEM)
    dma = pltpu.SemaphoreType.DMA
    shape = jax.ShapeDtypeStruct
    bf = lambda *dims: pltpu.VMEM(dims, BF)
    f32 = lambda *dims: pltpu.VMEM(dims, F32)
    grad_inputs, grad_qkv, grad_out = pl.pallas_call(
        kernel,
        out_shape=[shape((2, 128, D), BF), shape((9, 3, 576), F32), shape((9, 576), F32)],
        in_specs=[vm] * 5,
        out_specs=[vm] * 3,
        scratch_shapes=[
            bf(16, BLK), bf(16, BLK), bf(16, PW), bf(16, RW), bf(256, D), bf(16, 16, 2 * D), bf(D, D),
            f32(256, 1), bf(XS, ZS, YS, 16, PW), bf(XS, ZS, YS, 16, RW), bf(2, 8, 2, 16, 2 * D),
            bf(D, D), bf(512, D), f32(1024, 128), bf(XS, ZS, YS, 16, PW), bf(XS, ZS, YS, 16, RW),
            bf(2, 256, D), bf(2, 128, D), bf(2, 128, D), bf(128, D), bf(8, 16, D), bf(8, 2, 16, D),
            bf(2, 2, 4, 16, PW), bf(2, 2, ZS, 16, PW), bf(2, 2, 4, 16, PW), bf(2, ZS, 16, PW),
            bf(ZS, 16, PW), bf(ZS, 16, PW), bf(7, 16, PW),
            bf(YS, ZS, 16, RW), bf(YS, ZS, 16, RW), bf(2, 4, 16, RW), bf(2, ZS, 16, RW),
            bf(2, 4, 16, RW), bf(ZS, 16, RW), bf(7, 16, RW), f32(16, BLK), f32(16, BLK),
            dma((88,)), dma((88,)), dma((8,)), dma((8,)), dma((2,)), dma((2,)), dma((2,)),
        ],
        compiler_params=pltpu.CompilerParams(
            collective_id=0, has_side_effects=True, vmem_limit_bytes=VMEM_BYTES
        ),
        name="sublayer_backward",
    )(inputs, out_grad, gate.reshape(1, D), qkv_weight, out_weight)
    return grad_inputs, grad_qkv, grad_out


def solution(mesh):
    in_specs = (
        P("seq", None, None),
        P("seq", None, None),
        P(),
        P("seq", None, "head"),
        P("seq", "head"),
    )
    out_specs = (P("seq", None, None), P("seq", None, "head"), P("seq", "head"))
    return jax.shard_map(
        on_device, mesh=mesh, in_specs=in_specs, out_specs=out_specs, check_vma=False
    )
```

time: 1750 us -> 109 us (0.06)
  waiting for transfers between devices: 1590 us -> 0 us
  Pallas kernels: 0 us -> 104 us
  local copies, waits for them, and re-layouts: 61 us -> 4.65 us
  blocking collectives: 46.8 us -> 0 us
  matrix products: 19.5 us -> 0 us
    unnamed x5 -> x0, waiting for transfers between devices: 1300 us -> none
    all_gather x2 -> x0, waiting for transfers between devices: 236 us -> none  [the longest x1 120 us: on_device(): lax.all_gather(out_weight, 'seq', axis=0, tiled=True)]
    pallas_call x0 -> x1, Pallas kernels: none -> 104 us  [on_device(): pl.pallas_call(kernel, out_shape=[shape((2, 128, D), BF), shape((9, 3, 57...]
    all_to_all x1 -> x0, blocking collectives: 46.8 us -> none  [on_device(): lax.all_to_all(jnp.concatenate([qkv, dout], 2), 'seq', split_axis=1, conc...]
    all_to_all x1 -> x0, waiting for transfers between devices: 36.9 us -> none  [on_device(): back = lax.all_to_all(grads, 'seq', split_axis=0, concat_axis=1, tiled=True)]
    dot_general x10 -> x0, matrix products: 17.9 us -> none  [the longest x1 4.66 us: finish_grads(): lax.dot_general(dqkv, w_flat, (((1,), (1,)), ((), ())), preferred_element...]
  transfers between devices with their start and end apart: 5 -> 0, of which waited for: 5 -> 0; matrix products, arithmetic and copies ran while one was open for 2% -> 0% of each run, Pallas kernels for 0% -> 0%
where the time goes in v3:
time: 109 us
  Pallas kernels  104 us (95%)
  local copies, waits for them, and re-layouts  4.65 us (4%)
    pallas_call x1, Pallas kernels, on_device(): pl.pallas_call(kernel, out_shape=[shape((2, 128, D), BF), shape((9, 3, 57...  104 us
    unnamed x7, local copies, waits for them, and re-layouts  3.36 us

profile of v3, /device:TPU:1, one launch (start us, length us, event | category | flops | bytes accessed | tf_op | source)
XLA Modules:
  0.0 109.0 jit_solution(16247491486482355800)
XLA Ops:
  0.6 1.3 %reshape.9.gate_ref = f32[1,1152]{1,0:T(1,128)} reshape(f32[1152]{0:T(1024)} %param.7) | data formatting | bytes 9216 | tf_op jit(solution)/shard_map/reshape | solution.py:468
  1.9 103.7 %sublayer_backward.1 = (bf16[2,128,1152]{2,1,0:T(8,128)(2,1)}, f32[9,3,576]{2,1,0:T(4,128)}, f32[9,576]{1,0:T(8,128)}) custom-call(bf16[2,128,1152]{2,1,0:T(8,128)(2,1)} %in_ref.1, bf16[2,128,1152]{2,1,0:T(8,128)(2,1)} %up_ref.1, f32[1,1152]{1,0:T(1,128)} %reshape.9.gate_ref, bf16[9,3,576]{2,1,0:T(4,128)(2,1)} %wq_ref.1, bf16[9,576]{1,0:T(8,128)(2,1)} %wo_ref.1), custom_call_target="tpu_custom_call" | custom-call | tf_op jit(solution)/shard_map/sublayer_backward/pallas_call | solution.py:448
  105.6 0.0 copy-start
  105.6 2.0 %copy.11 = bf16[2,128,1152]{2,1,0:T(8,128)(2,1)} copy(bf16[2,128,1152]{2,1,0:T(8,128)(2,1)} %get-tuple-element.6) | data formatting | bytes 1179648
  107.6 0.0 copy-done
  107.6 0.0 copy-start.1
  107.6 0.6 copy.12
  108.2 0.1 copy-done.1
  108.4 0.6 copy.13
Async XLA Ops:
  105.6 2.0 %copy-start = (f32[9,3,576]{2,1,0:T(4,128)S(1)}, f32[9,3,576]{2,1,0:T(4,128)}, u32[]{:S(2)}) copy-start(f32[9,3,576]{2,1,0:T(4,128)} %get-tuple-element.7) | copy-start | bytes 186628
  107.6 0.8 copy-start.1

commit v4 on v3

v4 whole, which is shorter than its diff:
```python
import functools

import jax
import jax.numpy as jnp
from jax import lax
from jax.experimental import pallas as pl
from jax.experimental.pallas import tpu as pltpu
from jax.sharding import PartitionSpec as P

D = 1152
HEAD_DIM = 72
XS, ZS, YS = 2, 8, 4
CHIPS = XS * ZS * YS
BLK = 1408
GP, SP = 512, 640
GW, SW = GP + BLK - D, SP + BLK - D
GQ, SQ = D - GP, D - SP
OFFS = (0, 7, 1, 6, 2, 5, 3, 4)
SLOT = tuple(OFFS.index(d) for d in range(8))
GROUPS = (pl.ds(0, 1), pl.ds(1, 2), pl.ds(3, 2), pl.ds(5, 3))
MESH = pl.DeviceIdType.MESH
BF = jnp.bfloat16
F32 = jnp.float32
VMEM_BYTES = 58 * 2**20


def place():
    s = lax.axis_index("seq")
    h = lax.axis_index("head")
    return s // 64, (s // 8) % 8, (s // 2) % 4, s % 2, h


def seq_of(x, z, y, core):
    return ((x * 8 + z) * 4 + y) * 2 + core


def signal(sem, target):
    pl.semaphore_signal(sem, inc=1, device_id=target, device_id_type=MESH)


def remote(src, dst, send, recv, target):
    return pltpu.make_async_remote_copy(
        src_ref=src, dst_ref=dst, send_sem=send, recv_sem=recv, device_id=target, device_id_type=MESH
    )


def permuted_feature(shape, dim):
    f = lax.broadcasted_iota(jnp.int32, shape, dim)
    owner = f // 9
    q = f - owner * 9
    return jnp.where(q < 8, owner * 8 + q, 1024 + (owner % 2) * 64 + owner // 2)


class Copies:
    def __init__(self, send, recv):
        self.send, self.recv, self.count = send, recv, 0

    def start(self, src, dst, target):
        k = self.count
        self.count += 1
        c = remote(src, dst, self.send.at[k], self.recv.at[k], target)
        c.start()
        return c


class RowSum:
    def __init__(self, net, src, far, got, both, up, down, by_up):
        self.net, self.src, self.far, self.got, self.both = net, src, far, got, both
        self.up, self.down, self.by_up = up, down, by_up

    def first(self):
        net, src = self.net, self.src
        if self.by_up:
            self.c = [net.start(src(2), self.far, self.up), net.start(src(3), self.got[1], self.down)]
        else:
            self.c = [net.start(src(2), self.far, self.down), net.start(src(1), self.got[0], self.up)]

    def second(self):
        self.c[0].wait_recv()
        t = self.src(1 if self.by_up else 3)[...].astype(F32) + self.far[...].astype(F32)
        self.both[...] = t.astype(BF)
        if self.by_up:
            self.c.append(self.net.start(self.both, self.got[0], self.up))
        else:
            self.c.append(self.net.start(self.both, self.got[1], self.down))

    def total(self):
        self.c[1].wait_recv()
        self.c[2].wait_recv()
        t = self.src(0)[...].astype(F32)
        return t + self.got[0][...].astype(F32) + self.got[1][...].astype(F32)

    def end(self):
        for c in self.c:
            c.wait_send()


def normalise(v):
    mean = jnp.mean(v, -1, keepdims=True)
    centered = v - mean
    rstd = lax.rsqrt(jnp.mean(centered * centered, -1, keepdims=True) + 1e-06)
    return centered * rstd, rstd


def turn(v, by):
    return jnp.concatenate([v[:, -by:], v[:, :-by]], 1)


def nt(a, b):
    return lax.dot_general(a, b, (((1,), (1,)), ((), ())), preferred_element_type=F32)


def tn(a, b):
    return lax.dot_general(a, b, (((0,), (0,)), ((), ())), preferred_element_type=F32)


def attention(qa, ka, va, da):
    scale = HEAD_DIM ** (-0.5)
    rows = lax.broadcasted_iota(jnp.int32, (256, 256), 0)
    cols = lax.broadcasted_iota(jnp.int32, (256, 256), 1)
    same = (rows & 7) == (cols & 7)
    outs = [[[] for _ in range(3)] for _ in range(4)]
    for head, (lo, hi) in enumerate(((0, 128), (0, 256), (128, 256), (128, 384))):
        lane = lax.broadcasted_iota(jnp.int32, (1, hi - lo), 1) + lo
        keep = (lane >= HEAD_DIM * head) & (lane < HEAD_DIM * (head + 1))
        q, k, v, d = (a[:, lo:hi] for a in (qa, ka, va, da))
        qm = jnp.where(keep, q, jnp.zeros_like(q))
        dm = jnp.where(keep, d, jnp.zeros_like(d))
        scores = jnp.where(same, nt(qm, k) * scale, -1e30)
        top = jnp.max(scores, -1, keepdims=True)
        e = jnp.exp(scores - top)
        probs = e / jnp.sum(e, -1, keepdims=True)
        probs_b = probs.astype(BF)
        att = jnp.dot(probs_b, v, preferred_element_type=F32).astype(BF)
        delta = jnp.sum(dm.astype(F32) * att.astype(F32), -1, keepdims=True)
        ds = (probs * (nt(dm, v) - delta) * scale).astype(BF)
        dq = jnp.dot(ds, k, preferred_element_type=F32)
        dk = tn(ds, q)
        dv = tn(probs_b, d)
        for slot, val in zip(outs, (dq, dk, dv, att.astype(F32))):
            val = jnp.where(keep, val, 0.0)
            for t in range(lo // 128, hi // 128):
                slot[t].append(val[:, t * 128 - lo : t * 128 - lo + 128])
    return [jnp.concatenate([functools.reduce(lambda a, b: a + b, t) for t in s], 1) for s in outs]


def kernel(
    in_hbm, up_hbm, gate_ref, wq_ref, wo_ref, out, gq, go,
    in_ref, up_ref, sib_v, away_v, mine_p, mine_q, nat_v, xg_v, perm_v, rstd_v, buf_p, buf_q, xin,
    w_v, g_v, f_v, dw_p, dw_q, dn, rs, ps, rh, res_v, og,
    far_p, got_p, both_p, pyp, rxp, pxp, rzp, rq, tq, zq, far_q, got_q, both_q, pq, rxq, fin_v, fsib_v,
    send_sem, recv_sem, o_send, o_recv, s_send, s_recv, l_sem,
):
    x, z, y, core, h = place()
    zl = z % 2
    ck = zl * 4 + y
    member = ck * 2 + core
    base = (x * 8 + (z // 2) * 2) * 8
    above, below, far = (y + 1) % 4, (y + 3) % 4, (y + 2) % 4
    sibling = (seq_of(x, z, y, 1 - core), h)
    x_peer = (seq_of(1 - x, z, y, core), h)
    h_peer = (seq_of(x, z, y, core), 1 - h)
    y_up = (seq_of(x, z, above, core), h)
    y_dn = (seq_of(x, z, below, core), h)
    z_up = (seq_of(x, (z + 1) % 8, y, core), h)
    z_dn = (seq_of(x, (z + 7) % 8, y, core), h)
    z_peers = [(seq_of(x, (z + d) % 8, y, core), h) for d in range(1, 8)]
    plane, other = pl.ds(zl * 4, 4), pl.ds((1 - zl) * 4, 4)
    zb = (z // 2) * 2
    near_peers = [(seq_of(x, z, yy, core), h) for yy in [(y + d) % 4 for d in range(1, 4)]]
    cross_peers = [(seq_of(x, zb + 1 - zl, yy, core), h) for yy in [(y + d) % 4 for d in range(4)]]
    group = [(base + (member + i) % 16, h) for i in range(1, 16)]
    everyone = [x_peer, h_peer] + z_peers + group
    net = Copies(send_sem, recv_sem)
    barrier = pltpu.get_barrier_semaphore()
    for peer in everyone:
        signal(barrier, peer)

    load = [
        pltpu.make_async_copy(in_hbm, in_ref, l_sem.at[2]),
        pltpu.make_async_copy(up_hbm, up_ref, l_sem.at[3]),
    ]
    for c in load:
        c.start()

    wq, wo = wq_ref[...].astype(F32), wo_ref[...].astype(F32)
    blocks = []
    for half in range(2):
        c = slice(288 * half, 288 * half + 288)
        rows = jnp.concatenate([wq[:, 0, c], wq[:, 1, c], wq[:, 2, c], wo[:, c]], 1)
        main, last = rows[0:8], rows[8:9]
        last = [last[:, 128 * j : 128 * j + 128] for j in range(9)] + [jnp.zeros((7, 128), F32)]
        last = jnp.concatenate(last, 0)
        main0 = jnp.concatenate([main, jnp.zeros((8, D), F32)], 0)
        main1 = jnp.concatenate([jnp.zeros((8, D), F32), main], 0)
        none = jnp.zeros((16, 128), F32)
        block0 = jnp.concatenate([main0, last, none], 1)
        block1 = jnp.concatenate([main1, none, last], 1)
        blocks.append(jnp.where(core == 0, block0, block1))
    away_v[...] = jnp.where(core == 0, blocks[1], blocks[0]).astype(BF)
    mine = jnp.where(core == 0, blocks[0], blocks[1])
    row = permuted_feature((D, 1), 0)
    col = lax.broadcasted_iota(jnp.int32, (1, D), 1)
    perm_v[...] = jnp.where(row == col, 1.0, 0.0).astype(BF)
    for c in load:
        c.wait()
    ghat, rstd = normalise(in_ref[...].reshape(256, D).astype(F32))
    rstd_v[...] = rstd
    nat_v[0] = ghat.astype(BF)
    nat_v[1] = (gate_ref[...].reshape(1, D) * up_ref[...].reshape(256, D).astype(F32)).astype(BF)
    pl.semaphore_wait(barrier, len(everyone))

    swap = net.start(away_v, sib_v, sibling)
    for i in range(2):
        p = jnp.dot(nat_v[i], perm_v[...], preferred_element_type=F32)
        for g in range(16):
            part = jnp.concatenate([p[8 * g : 8 * g + 8], p[128 + 8 * g : 136 + 8 * g]], 0)
            xg_v[g, :, i * D : (i + 1) * D] = part.astype(BF)
    swap.wait()
    mine = (mine + sib_v[...].astype(F32)).astype(BF)
    own_q = mine[:, GP:D]
    mine_p[:, 0:GP] = mine[:, :GP]
    mine_p[:, GP:GW] = mine[:, D:]
    mine_q[...] = own_q
    buf_p[x, 0, y, :, 0:GP] = mine[:, :GP]
    buf_p[x, 0, y, :, GP:GW] = mine[:, D:]
    buf_q[z, x, y] = own_q
    q_x = net.start(mine_q, buf_q.at[z, x, y], x_peer)
    sent = [{} for _ in GROUPS]

    def first(g):
        own = buf_p.at[x, GROUPS[g], y]
        for way, peer in (("up", y_up), ("dn", y_dn), ("x", x_peer)):
            sent[g][way] = net.start(own, own, peer)

    z_c = {}

    def z_send(d):
        z_c[d] = net.start(mine_p, buf_p.at[x, SLOT[8 - d], y], z_peers[d - 1])

    def arrived(g):
        for j in range(GROUPS[g].start, GROUPS[g].start + GROUPS[g].size):
            z_c[8 - OFFS[j]].wait_recv()

    def second(g):
        t = sent[g]
        t["up"].wait_recv()
        got = buf_p.at[x, GROUPS[g], below]
        t["f"] = net.start(got, got, y_up)
        t["x"].wait_recv()
        own = buf_p.at[1 - x, GROUPS[g], y]
        t["oup"] = net.start(own, own, y_up)
        t["odn"] = net.start(own, own, y_dn)

    def third(g):
        t = sent[g]
        t["odn"].wait_recv()
        got = buf_p.at[1 - x, GROUPS[g], above]
        t["of"] = net.start(got, got, y_dn)

    def pass_on(at, peer):
        return net.start(at, at, peer)

    tok, tok_z = {}, {}

    def tok_near(d):
        to = zl * 4 + (y + d) % 4
        tok[d] = net.start(xg_v.at[pl.ds(2 * to, 2)], xin.at[:, ck, core], near_peers[d - 1])

    def tok_cross(d):
        to = (1 - zl) * 4 + (y + d) % 4
        tok_z[d] = net.start(xg_v.at[2 * to + h], xin.at[h, ck, core], cross_peers[d])

    t_h = []

    def tok_share(d):
        tok_z[d].wait_recv()
        t_h.append(pass_on(xin.at[h, (1 - zl) * 4 + (y + 4 - d) % 4, core], h_peer))

    for d in (1, 7, 2, 6, 3, 5, 4):
        z_send(d)
    first(0)
    own_t = pltpu.make_async_copy(xg_v.at[pl.ds(2 * ck, 2)], xin.at[:, ck, core], l_sem.at[0])
    own_t.start()
    q_x.wait_recv()
    q_c = [pass_on(buf_q.at[z, :, y], y_up), pass_on(buf_q.at[z, :, y], y_dn)]
    arrived(1)
    first(1)
    q_c[0].wait_recv()
    q_f0 = pass_on(buf_q.at[z, 0, below], y_up)
    q_c[1].wait_recv()
    q_f1 = pass_on(buf_q.at[z, 1, above], y_dn)
    tok_cross(0)
    tok_cross(2)
    arrived(2)
    first(2)
    second(0)
    q_f0.wait_recv()
    q_f1.wait_recv()
    ring_up, ring_dn = [[], []], [[], []]
    for i in range(2):
        ring_up[i].append(pass_on(buf_q.at[z, i], z_up))
        ring_dn[i].append(pass_on(buf_q.at[z, i], z_dn))

    def ring(step):
        for i in range(2):
            ring_up[i][-1].wait_recv()
            if step < 3 or i == 0:
                ring_up[i].append(pass_on(buf_q.at[(z + 8 - step) % 8, i], z_up))
            ring_dn[i][-1].wait_recv()
            if step < 3 or i == 1:
                ring_dn[i].append(pass_on(buf_q.at[(z + step) % 8, i], z_dn))

    tok_cross(1)
    arrived(3)
    first(3)
    second(1)
    tok_near(1)
    tok_near(3)
    tok_share(0)
    tok_share(2)
    ring(1)
    tok_cross(3)
    third(0)
    second(2)
    third(1)
    tok_share(1)
    ring(2)
    second(3)
    tok_near(2)
    third(2)
    ring(3)
    tok_share(3)
    third(3)
    own_t.wait()
    for d in (1, 3, 2):
        tok[d].wait_recv()
    t_s = [pass_on(xin.at[:, plane, core], sibling)]
    for c in t_h:
        c.wait_recv()
    t_s.append(pass_on(xin.at[:, other, core], sibling))
    ring_up[0][-1].wait_recv()
    ring_dn[1][-1].wait_recv()
    for g, t in enumerate(sent):
        for name in ("dn", "f", "of", "oup"):
            t[name].wait_recv()
    for c in t_s:
        c.wait_recv()

    for xx in range(2):
        for j in range(8):
            k = pl.ds(pl.multiple_of((xx * 8 + (z + OFFS[j]) % 8) * 64, 64), 64)
            w_v[k, 0:GP] = buf_p[xx, j, :, :, 0:GP].reshape(64, GP)
        for zz in range(8):
            k = (xx * 8 + zz) * 64
            w_v[k : k + 64, GP:D] = buf_q[zz, xx].reshape(64, GQ)
    for r in range(2):
        for xx in range(2):
            for j in range(8):
                k = pl.ds(pl.multiple_of((xx * 8 + (z + OFFS[j]) % 8) * 64, 64), 64)
                part = buf_p[xx, j, :, :, GP + 128 * r : GP + 128 * (r + 1)]
                f_v[k, :] = part.reshape(64, 128).astype(F32)
        for j in range(9):
            w_v[1024 + 64 * r : 1088 + 64 * r, 128 * j : 128 * (j + 1)] = f_v[
                pl.ds(j, 64, stride=16), :
            ].astype(BF)

    lane = lax.broadcasted_iota(jnp.int32, (1, 896), 1)
    away = pl.ds(pl.multiple_of((1 - core) * 128, 128), 128)
    here = pl.ds(pl.multiple_of(core * 128, 128), 128)

    def swap_dn(pg):
        return remote(dn.at[pg, away], rs.at[pg], s_send.at[pg], s_recv.at[pg], sibling)

    def tokens(pg, carry):
        tok = pl.ds(pg * 256, 256)
        src = xin[pg].reshape(256, 2 * D)
        qkv = jnp.dot(src[:, :D], w_v[:, 0:896], preferred_element_type=F32)
        od = jnp.dot(src[:, D:], w_v[:, 768:1152], preferred_element_type=F32)
        qa = qkv[:, 0:384].astype(BF)
        ka = turn(qkv[:, 256:640], -32).astype(BF)
        va = turn(qkv[:, 512:896], -64).astype(BF)
        da = turn(od, -96).astype(BF)
        dq, dk, dv, att = attention(qa, ka, va, da)
        dk, dv, att = turn(dk, 32), turn(dv, 64), turn(att, 96)
        tiles = [[] for _ in range(9)]
        for start, val in ((0, dq), (2, dk), (4, dv), (6, att)):
            for t in range(3):
                tiles[start + t].append(val[:, 128 * t : 128 * (t + 1)])
        for t in range(9):
            g_v[tok, 128 * t : 128 * (t + 1)] = functools.reduce(lambda a, b: a + b, tiles[t]).astype(BF)
        left = jnp.where(lane < 864, g_v[tok, 0:896], jnp.zeros((256, 896), BF))
        dn[pg] = nt(left, w_v[:, 0:896]).astype(BF)
        swap_dn(pg).start()
        return carry

    lax.fori_loop(0, 2, tokens, 0)

    def grads(i):
        a = tn(xin[:, :, :, :, pl.ds(pl.multiple_of(128 * i, 128), 128)].reshape(512, 128), g_v[:, 0:896])
        b = tn(
            xin[:, :, :, :, pl.ds(pl.multiple_of(D + 128 * i, 128), 128)].reshape(512, 128),
            g_v[:, 768:1152],
        )
        lane = lax.broadcasted_iota(jnp.int32, (1, 128), 1)
        mid = jnp.where(lane < 96, a[:, 768:896], b[:, 0:128])
        return jnp.concatenate([a[:, 0:768], mid, b[:, 128:384]], 1)

    def grad_rows(i, carry):
        block = grads(i).astype(BF).reshape(2, 4, 16, D)
        xx = i // 4
        for e in range(2):
            zz = 2 * (i % 4) + e
            o = (zz + 8 - z) % 8
            slot = (o // 4) * (15 - 4 * o) + 2 * o
            dw_p[xx, slot, :, :, 0:SP] = block[e, :, :, :SP]
            dw_q[zz, xx] = block[e, :, :, SP:]
        return carry

    lax.fori_loop(0, 8, grad_rows, 0)

    def q_own(o):
        return dw_q.at[(z + o) % 8]

    q_ring = {(0, 0): [net.start(dw_q.at[(z + 4) % 8, 0], rq.at[0, 0, 0], z_up)]}
    q_ring[1, 1] = [net.start(dw_q.at[(z + 4) % 8, 1], rq.at[1, 0, 1], z_dn)]
    for i, o, peer in ((0, 3, z_up), (1, 5, z_dn)):
        q_ring[i, 1 - i] = [net.start(dw_q.at[(z + o) % 8, 1 - i], rq.at[i, 1, 1 - i], peer)]

    def q_step(s):
        for i, o, peer in ((0, 4 - s, z_up), (1, 4 + s, z_dn)):
            for half in (i, 1 - i):
                if s == 1 and half != i:
                    continue
                q_ring[i, half][-1].wait_recv()
                t = q_own(o)[half].astype(F32) + rq[i, s - 1, half].astype(F32)
                tq[i, s - 1, half] = t.astype(BF)
                q_ring[i, half].append(net.start(tq.at[i, s - 1, half], rq.at[i, s, half], peer))

    for pg in range(2):
        swap_dn(pg).wait_recv()
    ps[...] = (dn[:, here].astype(F32) + rs[...].astype(F32)).astype(BF)
    dn_h = net.start(ps.at[1 - h], rh, h_peer)

    rest = grads(8)
    for r in range(2):
        f_v[...] = jnp.zeros((1024, 128), F32)
        for j in range(9):
            f_v[pl.ds(j, 64, stride=16), :] = rest[64 * r : 64 * r + 64, 128 * j : 128 * (j + 1)]
        for xx in range(2):
            for j in range(8):
                k = pl.ds(pl.multiple_of((xx * 8 + (z + OFFS[j]) % 8) * 64, 64), 64)
                dw_p[xx, j, :, :, SP + 128 * r : SP + 128 * (r + 1)] = (
                    f_v[k, :].astype(BF).reshape(4, 16, 128)
                )

    sums = {}
    for g in (3, 2, 1, 0):
        for i, xx in enumerate((1 - x, x)):
            at = GROUPS[g]
            sums[g, i] = RowSum(
                net, (lambda d, xx=xx, at=at: dw_p.at[xx, at, (y + d) % 4]),
                far_p.at[i, at], (got_p.at[i, 0, at], got_p.at[i, 1, at]), both_p.at[i, at],
                y_up, y_dn, i == 0,
            )

    def y_first(g):
        for i in range(2):
            sums[g, i].first()

    def y_second(g):
        for i in range(2):
            sums[g, i].second()

    x_c, z_s = {}, {}

    def y_total(g):
        at = GROUPS[g]
        pyp[0, at] = sums[g, 0].total().astype(BF)
        x_c[g] = net.start(pyp.at[0, at], rxp.at[at], x_peer)
        pyp[1, at] = sums[g, 1].total().astype(BF)

    def x_total(g):
        at = GROUPS[g]
        x_c[g].wait_recv()
        pxp[at] = (pyp[1, at].astype(F32) + rxp[at].astype(F32)).astype(BF)
        for j in range(at.start, at.start + at.size):
            if j:
                z_s[j] = net.start(pxp.at[j], rzp.at[j - 1], z_peers[OFFS[j] - 1])

    y_first(3)
    y_first(2)
    q_step(1)
    y_second(3)
    y_first(1)
    q_step(2)
    dn_h.wait_recv()
    mine = ps[h].astype(F32) + rh[...].astype(F32)
    mine = mine.astype(BF).astype(F32)
    ghat = xin[h, pl.ds(4 * core, 4), :, :, 0:D].reshape(128, D).astype(F32)
    one = jnp.mean(mine, -1, keepdims=True)
    two = jnp.mean(mine * ghat, -1, keepdims=True)
    res_v[...] = (mine - one - ghat * two).astype(BF).reshape(8, 16, D)

    local = zl == core

    def owner(i):
        to = (member + i) % 8
        target = (base + 8 * core + to, h)
        return remote(res_v.at[to], og.at[ck, h], o_send.at[i], o_recv.at[ck], target)

    stay = pltpu.make_async_copy(res_v.at[member % 8], og.at[ck, h], l_sem.at[1])
    pl.when(jnp.logical_not(local))(lambda: owner(0).start())
    pl.when(local)(lambda: stay.start())
    for i in range(1, 8):
        owner(i).start()

    y_second(2)
    y_total(3)
    y_first(0)
    y_second(1)
    q_step(3)
    y_total(2)
    x_total(3)
    y_second(0)

    def out_share(part):
        for c in range(4 * part, 4 * part + 4):
            got = remote(res_v.at[0], og.at[c, h], o_send.at[0], o_recv.at[c], h_peer)
            pl.when(jnp.logical_not(local & (ck == c)))(lambda got=got: got.wait_recv())
            pl.when(local & (ck == c))(lambda: stay.wait())
        at = og.at[pl.ds(4 * part, 4), h]
        return net.start(at, at, h_peer)

    y_total(1)
    o_h = [out_share(0)]
    x_total(2)
    y_total(0)
    o_h.append(out_share(1))
    for c in q_ring.values():
        c[-1].wait_recv()
    t = q_own(0)[...].astype(F32) + rq[0, 3].astype(F32) + rq[1, 3].astype(F32)
    zq[...] = t.astype(BF)
    q_sums = []
    for i in range(2):
        at = pl.ds(i, 1)
        q_sums.append(
            RowSum(
                net, (lambda d, at=at: zq.at[at, (y + d) % 4]),
                far_q.at[at], (got_q.at[0, at], got_q.at[1, at]), both_q.at[at],
                y_up, y_dn, i == 0,
            )
        )
        q_sums[i].first()
    x_total(1)
    for i in range(2):
        q_sums[i].second()
    x_total(0)
    for i in range(2):
        pq[i] = q_sums[i].total()[0].astype(BF)
    q_x2 = net.start(pq.at[1 - x], rxq, x_peer)

    for c in o_h:
        c.wait_recv()
    back = nt(og[...].reshape(256, D), perm_v[...])
    for f in range(2):
        nat = jnp.concatenate([back[16 * g + 8 * f : 16 * g + 8 * f + 8] for g in range(16)], 0)
        nat = up_ref[f].astype(F32) + rstd_v[128 * f : 128 * f + 128] * nat
        out[f] = nat.astype(BF)

    t = pxp[0].astype(F32)
    for j in range(1, 8):
        z_s[j].wait_recv()
        t = t + rzp[j - 1].astype(F32)
    fin_v[:, 0:SP] = t[:, :SP]
    fin_v[:, D:BLK] = t[:, SP:]
    q_x2.wait_recv()
    fin_v[:, SP:D] = pq[x].astype(F32) + rxq[...].astype(F32)
    last = net.start(fin_v, fsib_v, sibling)
    last.wait()

    mine, other = fin_v[...], fsib_v[...]
    rows = []
    for half in (jnp.where(core == 0, mine, other), jnp.where(core == 0, other, mine)):
        main = jnp.where(core == 0, half[0:8, :D], half[8:16, :D])
        tail = jnp.where(core == 0, half[0:9, D : D + 128], half[0:9, D + 128 :])
        tail = jnp.concatenate([tail[j : j + 1] for j in range(9)], 1)
        rows.append(jnp.concatenate([main, tail], 0))
    for t in range(4):
        both = jnp.concatenate([r[:, 288 * t : 288 * t + 288] for r in rows], 1)
        if t < 3:
            gq[:, t, :] = both
        else:
            go[...] = both

    pl.when(jnp.logical_not(local))(lambda: owner(0).wait_send())
    for i in range(1, 8):
        owner(i).wait_send()
    for pg in range(2):
        swap_dn(pg).wait_send()
    for t in sent:
        for c in t.values():
            c.wait_send()
    rest = o_h + [q_x, q_f0, q_f1, dn_h, q_x2] + q_c + t_h + t_s
    for c in ring_up + ring_dn + list(q_ring.values()):
        rest = rest + c
    for c in rest + list(tok.values()) + list(tok_z.values()) + list(z_c.values()) + list(x_c.values()) + list(z_s.values()):
        c.wait_send()
    for c in q_sums + list(sums.values()):
        c.end()


def on_device(inputs, out_grad, gate, qkv_weight, out_weight):
    vm = pl.BlockSpec(memory_space=pltpu.VMEM)
    hbm = pl.BlockSpec(memory_space=pl.ANY)
    dma = pltpu.SemaphoreType.DMA
    shape = jax.ShapeDtypeStruct
    bf = lambda *dims: pltpu.VMEM(dims, BF)
    f32 = lambda *dims: pltpu.VMEM(dims, F32)
    grad_inputs, grad_qkv, grad_out = pl.pallas_call(
        kernel,
        out_shape=[shape((2, 128, D), BF), shape((9, 3, 576), F32), shape((9, 576), F32)],
        in_specs=[hbm] * 2 + [vm] * 3,
        out_specs=[vm] * 3,
        scratch_shapes=[
            bf(2, 128, D), bf(2, 128, D),
            bf(16, BLK), bf(16, BLK), bf(16, GW), bf(16, GQ), bf(2, 256, D), bf(16, 16, 2 * D), bf(D, D),
            f32(256, 1), bf(XS, ZS, YS, 16, GW), bf(ZS, XS, YS, 16, GQ), bf(2, 8, 2, 16, 2 * D),
            bf(D, D), bf(512, D), f32(1024, 128), bf(XS, ZS, YS, 16, SW), bf(ZS, XS, YS, 16, SQ),
            bf(2, 256, D), bf(2, 128, D), bf(2, 128, D), bf(128, D), bf(8, 16, D), bf(8, 2, 16, D),
            bf(2, ZS, 16, SW), bf(2, 2, ZS, 16, SW), bf(2, ZS, 16, SW), bf(2, ZS, 16, SW),
            bf(ZS, 16, SW), bf(ZS, 16, SW), bf(7, 16, SW),
            bf(2, 4, XS, YS, 16, SQ), bf(2, 3, XS, YS, 16, SQ), bf(XS, YS, 16, SQ),
            bf(2, 16, SQ), bf(2, 2, 16, SQ), bf(2, 16, SQ), bf(2, 16, SQ), bf(16, SQ),
            f32(16, BLK), f32(16, BLK),
            dma((150,)), dma((150,)), dma((8,)), dma((8,)), dma((2,)), dma((2,)), dma((4,)),
        ],
        compiler_params=pltpu.CompilerParams(
            collective_id=0, has_side_effects=True, vmem_limit_bytes=VMEM_BYTES
        ),
        name="sublayer_backward",
    )(inputs, out_grad, gate, qkv_weight, out_weight)
    return grad_inputs, grad_qkv, grad_out


def solution(mesh):
    in_specs = (
        P("seq", None, None),
        P("seq", None, None),
        P(),
        P("seq", None, "head"),
        P("seq", "head"),
    )
    out_specs = (P("seq", None, None), P("seq", None, "head"), P("seq", "head"))
    return jax.shard_map(
        on_device, mesh=mesh, in_specs=in_specs, out_specs=out_specs, check_vma=False
    )
```

time: 109 us -> 100 us (0.917)
  Pallas kernels: 104 us -> 96.1 us
  local copies, waits for them, and re-layouts: 4.65 us -> 3.36 us
    pallas_call x1, Pallas kernels: 104 us -> 96.1 us  [on_device(): pl.pallas_call(kernel, out_shape=[shape((2, 128, D), BF), shape((9, 3, 57...]
    reshape x1 -> x0, local copies, waits for them, and re-layouts: 1.29 us -> none  [on_device(): gate.reshape(1, D)]
where the time goes in v4:
time: 100 us
  Pallas kernels  96.1 us (96%)
  local copies, waits for them, and re-layouts  3.36 us (3%)
    pallas_call x1, Pallas kernels, on_device(): pl.pallas_call(kernel, out_shape=[shape((2, 128, D), BF), shape((9, 3, 57...  96.1 us
    unnamed x7, local copies, waits for them, and re-layouts  3.36 us

profile of v4, /device:TPU:1, one launch (start us, length us, event | category | flops | bytes accessed | tf_op | source)
XLA Modules:
  0.0 100.1 jit_solution(6077066828600364344)
XLA Ops:
  0.6 96.1 %sublayer_backward.1 = (bf16[2,128,1152]{2,1,0:T(8,128)(2,1)}, f32[9,3,576]{2,1,0:T(4,128)}, f32[9,576]{1,0:T(8,128)}) custom-call(bf16[2,128,1152]{2,1,0:T(8,128)(2,1)} %in_hbm.1, bf16[2,128,1152]{2,1,0:T(8,128)(2,1)} %up_hbm.1, f32[1152]{0:T(1024)} %gate_ref.1, bf16[9,3,576]{2,1,0:T(4,128)(2,1)} %wq_ref.1, bf16[9,576]{1,0:T(8,128)(2,1)} %wo_ref.1), custom_call_target="tpu_custom_call" | custom-call | tf_op jit(solution)/shard_map/sublayer_backward/pallas_call | solution.py:620
  96.7 0.0 copy-start
  96.7 2.0 %copy.11 = bf16[2,128,1152]{2,1,0:T(8,128)(2,1)} copy(bf16[2,128,1152]{2,1,0:T(8,128)(2,1)} %get-tuple-element.6) | data formatting | bytes 1179648
  98.7 0.0 copy-done
  98.7 0.0 copy-start.1
  98.7 0.6 copy.12
  99.3 0.1 copy-done.1
  99.5 0.6 copy.13
Async XLA Ops:
  96.7 2.0 %copy-start = (f32[9,3,576]{2,1,0:T(4,128)S(1)}, f32[9,3,576]{2,1,0:T(4,128)}, u32[]{:S(2)}) copy-start(f32[9,3,576]{2,1,0:T(4,128)} %get-tuple-element.7) | copy-start | bytes 186628
  98.7 0.8 copy-start.1

commit v5 on v4

--- a/solution.py
+++ b/solution.py
@@ -9,6 +9,7 @@
 
 D = 1152
 HEAD_DIM = 72
+LOG2E = 1.4426950408889634
 XS, ZS, YS = 2, 8, 4
 CHIPS = XS * ZS * YS
 BLK = 1408
@@ -124,19 +125,20 @@
         lane = lax.broadcasted_iota(jnp.int32, (1, hi - lo), 1) + lo
         keep = (lane >= HEAD_DIM * head) & (lane < HEAD_DIM * (head + 1))
         q, k, v, d = (a[:, lo:hi] for a in (qa, ka, va, da))
-        qm = jnp.where(keep, q, jnp.zeros_like(q))
-        dm = jnp.where(keep, d, jnp.zeros_like(d))
-        scores = jnp.where(same, nt(qm, k) * scale, -1e30)
-        top = jnp.max(scores, -1, keepdims=True)
-        e = jnp.exp(scores - top)
-        probs = e / jnp.sum(e, -1, keepdims=True)
+        km = jnp.where(keep, k, jnp.zeros_like(k))
+        vm = jnp.where(keep, v, jnp.zeros_like(v))
+        scores = jnp.where(same, nt(km, q), -1e30)
+        top = jnp.max(scores, 0, keepdims=True)
+        e = jnp.exp2((scores - top) * (scale * LOG2E))
+        probs = e * (1.0 / jnp.sum(e, 0, keepdims=True))
         probs_b = probs.astype(BF)
-        att = jnp.dot(probs_b, v, preferred_element_type=F32).astype(BF)
-        delta = jnp.sum(dm.astype(F32) * att.astype(F32), -1, keepdims=True)
-        ds = (probs * (nt(dm, v) - delta) * scale).astype(BF)
-        dq = jnp.dot(ds, k, preferred_element_type=F32)
-        dk = tn(ds, q)
-        dv = tn(probs_b, d)
+        att = tn(probs_b, v).astype(BF)
+        dprobs = nt(vm, d)
+        delta = jnp.sum(probs_b.astype(F32) * dprobs, 0, keepdims=True)
+        ds = (probs * (dprobs - delta) * scale).astype(BF)
+        dq = tn(ds, k)
+        dk = jnp.dot(ds, q, preferred_element_type=F32)
+        dv = jnp.dot(probs_b, d, preferred_element_type=F32)
         for slot, val in zip(outs, (dq, dk, dv, att.astype(F32))):
             val = jnp.where(keep, val, 0.0)
             for t in range(lo // 128, hi // 128):
@@ -312,6 +314,7 @@
                 ring_dn[i].append(pass_on(buf_q.at[(z + step) % 8, i], z_dn))
 
     tok_cross(1)
+    tok_cross(3)
     arrived(3)
     first(3)
     second(1)
@@ -320,25 +323,24 @@
     tok_share(0)
     tok_share(2)
     ring(1)
-    tok_cross(3)
     third(0)
     second(2)
+    tok_near(2)
+    tok_share(1)
+    tok_share(3)
     third(1)
-    tok_share(1)
     ring(2)
     second(3)
-    tok_near(2)
-    third(2)
-    ring(3)
-    tok_share(3)
-    third(3)
     own_t.wait()
     for d in (1, 3, 2):
         tok[d].wait_recv()
     t_s = [pass_on(xin.at[:, plane, core], sibling)]
+    third(2)
     for c in t_h:
         c.wait_recv()
     t_s.append(pass_on(xin.at[:, other, core], sibling))
+    ring(3)
+    third(3)
     ring_up[0][-1].wait_recv()
     ring_dn[1][-1].wait_recv()
     for g, t in enumerate(sent):
@@ -372,8 +374,8 @@
     def swap_dn(pg):
         return remote(dn.at[pg, away], rs.at[pg], s_send.at[pg], s_recv.at[pg], sibling)
 
-    def tokens(pg, carry):
-        tok = pl.ds(pg * 256, 256)
+    def tokens(pg):
+        tok = slice(pg * 256, pg * 256 + 256)
         src = xin[pg].reshape(256, 2 * D)
         qkv = jnp.dot(src[:, :D], w_v[:, 0:896], preferred_element_type=F32)
         od = jnp.dot(src[:, D:], w_v[:, 768:1152], preferred_element_type=F32)
@@ -389,12 +391,9 @@
                 tiles[start + t].append(val[:, 128 * t : 128 * (t + 1)])
         for t in range(9):
             g_v[tok, 128 * t : 128 * (t + 1)] = functools.reduce(lambda a, b: a + b, tiles[t]).astype(BF)
-        left = jnp.where(lane < 864, g_v[tok, 0:896], jnp.zeros((256, 896), BF))
-        dn[pg] = nt(left, w_v[:, 0:896]).astype(BF)
-        swap_dn(pg).start()
-        return carry
-
-    lax.fori_loop(0, 2, tokens, 0)
+
+    tokens(0)
+    tokens(1)
 
     def grads(i):
         a = tn(xin[:, :, :, :, pl.ds(pl.multiple_of(128 * i, 128), 128)].reshape(512, 128), g_v[:, 0:896])
@@ -436,11 +435,6 @@
                 t = q_own(o)[half].astype(F32) + rq[i, s - 1, half].astype(F32)
                 tq[i, s - 1, half] = t.astype(BF)
                 q_ring[i, half].append(net.start(tq.at[i, s - 1, half], rq.at[i, s, half], peer))
-
-    for pg in range(2):
-        swap_dn(pg).wait_recv()
-    ps[...] = (dn[:, here].astype(F32) + rs[...].astype(F32)).astype(BF)
-    dn_h = net.start(ps.at[1 - h], rh, h_peer)
 
     rest = grads(8)
     for r in range(2):
@@ -488,12 +482,27 @@
             if j:
                 z_s[j] = net.start(pxp.at[j], rzp.at[j - 1], z_peers[OFFS[j] - 1])
 
+    def partial_dn(pg):
+        left = jnp.where(lane < 864, g_v[pg * 256 : pg * 256 + 256, 0:896], jnp.zeros((256, 896), BF))
+        dn[pg] = nt(left, w_v[:, 0:896]).astype(BF)
+        swap_dn(pg).start()
+
     y_first(3)
     y_first(2)
+    partial_dn(0)
+    partial_dn(1)
     q_step(1)
     y_second(3)
     y_first(1)
+    for pg in range(2):
+        swap_dn(pg).wait_recv()
+    ps[...] = (dn[:, here].astype(F32) + rs[...].astype(F32)).astype(BF)
+    dn_h = net.start(ps.at[1 - h], rh, h_peer)
     q_step(2)
+    y_second(2)
+    y_total(3)
+    y_first(0)
+    y_second(1)
     dn_h.wait_recv()
     mine = ps[h].astype(F32) + rh[...].astype(F32)
     mine = mine.astype(BF).astype(F32)
@@ -515,10 +524,6 @@
     for i in range(1, 8):
         owner(i).start()
 
-    y_second(2)
-    y_total(3)
-    y_first(0)
-    y_second(1)
     q_step(3)
     y_total(2)
     x_total(3)

time: 100 us -> 96.1 us (0.961)
  Pallas kernels: 96.1 us -> 91.8 us
    pallas_call x1, Pallas kernels: 96.1 us -> 91.8 us  [on_device(): pl.pallas_call(kernel, out_shape=[shape((2, 128, D), BF), shape((9, 3, 57...]
where the time goes in v5:
time: 96.1 us; the launch traced here: 95.8 us
  Pallas kernels  91.8 us (96%)
  local copies, waits for them, and re-layouts  3.36 us (3%)
    pallas_call x1, Pallas kernels, on_device(): pl.pallas_call(kernel, out_shape=[shape((2, 128, D), BF), shape((9, 3, 57...  91.8 us
    unnamed x7, local copies, waits for them, and re-layouts  3.36 us

profile of v5, /device:TPU:1, one launch (start us, length us, event | category | flops | bytes accessed | tf_op | source)
XLA Modules:
  0.0 95.8 jit_solution(8774853138038582902)
XLA Ops:
  0.6 91.8 %sublayer_backward.1 = (bf16[2,128,1152]{2,1,0:T(8,128)(2,1)}, f32[9,3,576]{2,1,0:T(4,128)}, f32[9,576]{1,0:T(8,128)}) custom-call(bf16[2,128,1152]{2,1,0:T(8,128)(2,1)} %in_hbm.1, bf16[2,128,1152]{2,1,0:T(8,128)(2,1)} %up_hbm.1, f32[1152]{0:T(1024)} %gate_ref.1, bf16[9,3,576]{2,1,0:T(4,128)(2,1)} %wq_ref.1, bf16[9,576]{1,0:T(8,128)(2,1)} %wo_ref.1), custom_call_target="tpu_custom_call" | custom-call | tf_op jit(solution)/shard_map/sublayer_backward/pallas_call | solution.py:625
  92.5 0.0 copy-start
  92.5 2.0 %copy.11 = bf16[2,128,1152]{2,1,0:T(8,128)(2,1)} copy(bf16[2,128,1152]{2,1,0:T(8,128)(2,1)} %get-tuple-element.6) | data formatting | bytes 1179648
  94.4 0.0 copy-done
  94.4 0.0 copy-start.1
  94.4 0.6 copy.12
  95.1 0.1 copy-done.1
  95.2 0.6 copy.13
Async XLA Ops:
  92.5 2.0 %copy-start = (f32[9,3,576]{2,1,0:T(4,128)S(1)}, f32[9,3,576]{2,1,0:T(4,128)}, u32[]{:S(2)}) copy-start(f32[9,3,576]{2,1,0:T(4,128)} %get-tuple-element.7) | copy-start | bytes 186628
  94.4 0.8 copy-start.1

commit v6 on v5

--- a/solution.py
+++ b/solution.py
@@ -341,21 +341,13 @@
     t_s.append(pass_on(xin.at[:, other, core], sibling))
     ring(3)
     third(3)
-    ring_up[0][-1].wait_recv()
-    ring_dn[1][-1].wait_recv()
     for g, t in enumerate(sent):
         for name in ("dn", "f", "of", "oup"):
             t[name].wait_recv()
-    for c in t_s:
-        c.wait_recv()
-
     for xx in range(2):
         for j in range(8):
             k = pl.ds(pl.multiple_of((xx * 8 + (z + OFFS[j]) % 8) * 64, 64), 64)
             w_v[k, 0:GP] = buf_p[xx, j, :, :, 0:GP].reshape(64, GP)
-        for zz in range(8):
-            k = (xx * 8 + zz) * 64
-            w_v[k : k + 64, GP:D] = buf_q[zz, xx].reshape(64, GQ)
     for r in range(2):
         for xx in range(2):
             for j in range(8):
@@ -366,6 +358,14 @@
             w_v[1024 + 64 * r : 1088 + 64 * r, 128 * j : 128 * (j + 1)] = f_v[
                 pl.ds(j, 64, stride=16), :
             ].astype(BF)
+    ring_up[0][-1].wait_recv()
+    ring_dn[1][-1].wait_recv()
+    for xx in range(2):
+        for zz in range(8):
+            k = (xx * 8 + zz) * 64
+            w_v[k : k + 64, GP:D] = buf_q[zz, xx].reshape(64, GQ)
+    for c in t_s:
+        c.wait_recv()
 
     lane = lax.broadcasted_iota(jnp.int32, (1, 896), 1)
     away = pl.ds(pl.multiple_of((1 - core) * 128, 128), 128)
@@ -565,14 +565,6 @@
         pq[i] = q_sums[i].total()[0].astype(BF)
     q_x2 = net.start(pq.at[1 - x], rxq, x_peer)
 
-    for c in o_h:
-        c.wait_recv()
-    back = nt(og[...].reshape(256, D), perm_v[...])
-    for f in range(2):
-        nat = jnp.concatenate([back[16 * g + 8 * f : 16 * g + 8 * f + 8] for g in range(16)], 0)
-        nat = up_ref[f].astype(F32) + rstd_v[128 * f : 128 * f + 128] * nat
-        out[f] = nat.astype(BF)
-
     t = pxp[0].astype(F32)
     for j in range(1, 8):
         z_s[j].wait_recv()
@@ -582,6 +574,14 @@
     q_x2.wait_recv()
     fin_v[:, SP:D] = pq[x].astype(F32) + rxq[...].astype(F32)
     last = net.start(fin_v, fsib_v, sibling)
+    for c in o_h:
+        c.wait_recv()
+    back = nt(og[...].reshape(256, D), perm_v[...])
+    for f in range(2):
+        nat = jnp.concatenate([back[16 * g + 8 * f : 16 * g + 8 * f + 8] for g in range(16)], 0)
+        nat = up_ref[f].astype(F32) + rstd_v[128 * f : 128 * f + 128] * nat
+        out[f] = nat.astype(BF)
+
     last.wait()
 
     mine, other = fin_v[...], fsib_v[...]

time: 96.1 us -> 95.5 us (level)
  no operation moved by 1% of the time
where the time goes in v6:
time: 95.5 us; the launch traced here: 95.2 us
  Pallas kernels  91.2 us (95%)
  local copies, waits for them, and re-layouts  3.36 us (4%)
    pallas_call x1, Pallas kernels, on_device(): pl.pallas_call(kernel, out_shape=[shape((2, 128, D), BF), shape((9, 3, 57...  91.2 us
    unnamed x7, local copies, waits for them, and re-layouts  3.36 us

profile of v6, /device:TPU:1, one launch (start us, length us, event | category | flops | bytes accessed | tf_op | source)
XLA Modules:
  0.0 95.2 jit_solution(6291915871888754681)
XLA Ops:
  0.6 91.2 %sublayer_backward.1 = (bf16[2,128,1152]{2,1,0:T(8,128)(2,1)}, f32[9,3,576]{2,1,0:T(4,128)}, f32[9,576]{1,0:T(8,128)}) custom-call(bf16[2,128,1152]{2,1,0:T(8,128)(2,1)} %in_hbm.1, bf16[2,128,1152]{2,1,0:T(8,128)(2,1)} %up_hbm.1, f32[1152]{0:T(1024)} %gate_ref.1, bf16[9,3,576]{2,1,0:T(4,128)(2,1)} %wq_ref.1, bf16[9,576]{1,0:T(8,128)(2,1)} %wo_ref.1), custom_call_target="tpu_custom_call" | custom-call | tf_op jit(solution)/shard_map/sublayer_backward/pallas_call | solution.py:625
  91.8 0.0 copy-start
  91.9 2.0 %copy.11 = bf16[2,128,1152]{2,1,0:T(8,128)(2,1)} copy(bf16[2,128,1152]{2,1,0:T(8,128)(2,1)} %get-tuple-element.6) | data formatting | bytes 1179648
  93.8 0.0 copy-done
  93.8 0.0 copy-start.1
  93.8 0.6 copy.12
  94.5 0.1 copy-done.1
  94.6 0.6 copy.13
Async XLA Ops:
  91.8 2.0 %copy-start = (f32[9,3,576]{2,1,0:T(4,128)S(1)}, f32[9,3,576]{2,1,0:T(4,128)}, u32[]{:S(2)}) copy-start(f32[9,3,576]{2,1,0:T(4,128)} %get-tuple-element.7) | copy-start | bytes 186628
  93.8 0.8 copy-start.1
